TPU v7x, 256 devices: a whole 4x4x8 slice. The times are simulated.
256 devices in a mesh: prow: 16 (over z, core), pcol: 16 (over y, x).
Axes of the slice: x: 4, y: 4, z: 8, core: 2. Of those that a mesh axis runs over, the one named last changes fastest.
Arguments:
- inverse_block: float32 [20480, 20480], P('prow', 'pcol'), may hold values from -6 to 6
- l_panel: float32 [20480, 512], P(('prow', 'pcol')), may hold values from -0.0625 to 0.0625
- d_inverse: float32 [2, 256, 256], replicated, may hold values from -6 to 6
- owner_map: int32 [80], replicated, may hold values from 0 to 79, each once
- ancestors: int32 [2, 40], replicated, may hold values from 0 to 79, as said below
Outputs:
- inverse_column: float32 [20480, 512], P(('prow', 'pcol'))
- diag_inverse: float32 [2, 256, 256], replicated
Inputs may be any that keep to these rules, and one draw needn't show every extreme that they name: `ancestors`: each row holds 40 different block numbers in rising order; the two rows together hold every block number exactly once. `owner_map`: each block number appears once.
All inputs are finite; a program needn't handle non-finite values.
Results may differ from a plain program's by a relative error of at most 0.000075.
Values sent between devices are 32-bit elements; how exact they have to be, the bound alone decides.
No kernel may reach another device: no remote copies, remote signals or barrier semaphores. Data moves between devices by JAX's collectives and lax.ppermute only.
A program may use at most 64 MiB of HBM per device.

v0:
```python
import jax
import jax.numpy as jnp
from jax import lax
from jax.sharding import PartitionSpec as P


def broadcast(block, axis, source):
    block = jnp.where(lax.axis_index(axis) == source, block, jnp.zeros_like(block))
    return lax.psum(block, axis)


def per_device(inverse_block, l_panel, d_inverse, owner_map, ancestors):
    block = d_inverse.shape[1]
    width = l_panel.shape[1]
    rows_dev = l_panel.shape[0]
    n_row = lax.axis_size("prow")
    n_col = lax.axis_size("pcol")
    total = rows_dev * n_row * n_col
    n_blocks = owner_map.shape[0]
    col_rows = total // n_col
    row_rows = total // n_row
    ratio = n_row // n_col
    prow_index = lax.axis_index("prow")
    pcol_index = lax.axis_index("pcol")
    in_set = jnp.any(owner_map[None, :, None] == ancestors[:, None, :], axis=2).astype(jnp.float32)

    def row_mask(start, count):
        block_index = (start + jnp.arange(count, dtype=jnp.int32)) // block
        onehot = (block_index[:, None] == jnp.arange(n_blocks, dtype=jnp.int32)[None, :]).astype(
            jnp.float32
        )
        return jnp.dot(
            onehot, in_set.T, precision=lax.Precision.HIGHEST, preferred_element_type=jnp.float32
        )

    def apply_mask(panel, mask):
        return (panel.reshape(panel.shape[0], 2, block) * mask[:, :, None]).reshape(
            panel.shape[0], width
        )

    row_panel = lax.all_gather(l_panel, "pcol", axis=0, tiled=True)
    pieces = broadcast(row_panel, "prow", pcol_index * ratio + 0)
    masked_cols = apply_mask(pieces, row_mask(pcol_index * col_rows, col_rows))
    row_start = prow_index * row_rows
    summed = lax.psum_scatter(
        -jnp.dot(
            inverse_block,
            masked_cols,
            precision=lax.Precision.HIGHEST,
            preferred_element_type=jnp.float32,
        ),
        "pcol",
        scatter_dimension=0,
        tiled=True,
    )
    column = apply_mask(summed, row_mask(row_start + pcol_index * rows_dev, rows_dev))
    summed_terms = lax.psum(
        jnp.einsum(
            "rkb,rkc->kbc",
            l_panel.reshape(l_panel.shape[0], 2, block),
            column.reshape(column.shape[0], 2, block),
            precision=lax.Precision.HIGHEST,
        ),
        ("prow", "pcol"),
    )
    return (column, d_inverse - summed_terms)


def solution(mesh):
    return jax.shard_map(
        per_device,
        mesh=mesh,
        in_specs=(P("prow", "pcol"), P(("prow", "pcol"), None), P(), P(), P()),
        out_specs=(P(("prow", "pcol"), None), P()),
        check_vma=False,
    )
```

profile of v0, /device:TPU:1, one launch (start us, length us, event | category | flops | bytes accessed | tf_op | source)
XLA Modules:
  0.0 558.2 jit_solution(13528799346158119056)
XLA Ops:
  7.2 0.0 all-gather.2.cloned.1.call-start
  7.2 0.7 all-gather.2.cloned.1.call-update
  7.9 0.0 all-reduce.3.cloned.1.call-start
  8.0 57.2 %all-gather.2.cloned.1.call-done = f32[1280,512]{1,0:T(8,128)} async-done(((f32[80,512]{1,0:T(8,128)}), f32[1280,512]{1,0:T(8,128)}) %all-gather.2.cloned.1.call-update) | async-done | bytes 2621456 | tf_op jit(solution)/shard_map/all_gather | solution.py:41
  65.2 1.8 broadcast_select_fusion
  67.0 0.0 copy-start.2
  67.0 0.0 copy-start.3
  67.0 0.0 all-reduce.3.cloned.1.call-update
  67.0 0.0 reduce-scatter.4.cloned.1.call-start
  67.1 0.6 copy-done.2
  67.7 0.0 copy-done.3
  67.7 0.1 compare_reduce_fusion
  67.8 0.9 fusion.2
  68.7 2.9 mul.34
  71.6 0.2 copy.33
  71.9 112.4 %all-reduce.3.cloned.1.call-done = f32[1280,512]{1,0:T(8,128)} async-done(((f32[1280,512]{1,0:T(8,128)}), f32[1280,512]{1,0:T(8,128)}) %all-reduce.3.cloned.1.call-update) | async-done | bytes 2621456 | tf_op jit(solution)/shard_map/psum | solution.py:9
  184.2 25.4 %fusion = f32[1280,512]{0,1:T(8,128)} fusion(f32[1280,1280]{1,0:T(8,128)} %param.5, f32[1280,512]{1,0:T(8,128)} %all-reduce.3.cloned.1.call-done, f32[1280,512]{1,0:T(8,128)S(1)} %bitcast.17), kind=kOutput, calls=%fused_computation.1 | convolution fusion | flops 10067640320 | bytes 14417920 | tf_op jit(solution)/shard_map/dot_general | solution.py:46
  209.6 3.2 copy.29
  212.8 0.0 copy-start
  212.8 0.0 copy-start.1
  212.8 0.0 reduce-scatter.4.cloned.1.call-update
  212.8 0.0 all-reduce.5.cloned.1.call-start
  212.9 0.2 fusion.8
  213.1 79.0 %reduce-scatter.4.cloned.1.call-done = f32[80,512]{1,0:T(8,128)} async-done(((f32[1280,512]{1,0:T(8,128)}), f32[80,512]{1,0:T(8,128)}) %reduce-scatter.4.cloned.1.call-update) | async-done | bytes 163856
  292.1 1.0 copy.30
  293.1 0.1 copy.23
  293.2 0.0 copy-done
  293.3 1.5 convolution_bitcast_fusion
  294.7 0.0 all-reduce.5.cloned.1.call-update
  294.8 0.0 copy-done.1
  294.8 0.2 copy.25
  295.0 0.8 copy.26
  295.8 253.8 %all-reduce.5.cloned.1.call-done = f32[2,256,256]{1,2,0:T(8,128)} async-done(((f32[2,256,256]{1,2,0:T(8,128)}), f32[2,256,256]{1,2,0:T(8,128)}) %all-reduce.5.cloned.1.call-update) | async-done | bytes 524304 | tf_op jit(solution)/shard_map/psum | solution.py:57
  549.6 1.1 sub.17
  550.7 1.0 copy.27
  (3 shorter events, 0.0 us)
Async XLA Ops:
  7.2 58.0 %all-gather.2.cloned.1.call-start = ((), (), s32[]{:S(2)}) async-start(), calls=%async_computation.1 | async-start | bytes 2785280 | tf_op jit(solution)/shard_map/all_gather | solution.py:41
  7.9 176.3 %all-reduce.3.cloned.1.call-start = ((), (), s32[]{:S(2)}) async-start(), calls=%async_computation.2 | async-start | bytes 5242880 | tf_op jit(solution)/shard_map/psum | solution.py:9
  67.0 0.7 copy-start.2
  67.0 0.7 copy-start.3
  67.0 225.0 %reduce-scatter.4.cloned.1.call-start = ((), (), s32[]{:S(2)}) async-start(), calls=%async_computation.4 | async-start | bytes 2785280
  212.8 80.4 %copy-start = (f32[80,512]{1,0:T(8,128)S(1)}, f32[80,512]{1,0:T(8,128)}, u32[]{:S(2)}) copy-start(f32[80,512]{1,0:T(8,128)} %param.6) | copy-start | bytes 491524
  212.8 82.0 %copy-start.1 = (f32[2,256,256]{2,1,0:T(8,128)S(1)}, f32[2,256,256]{2,1,0:T(8,128)}, u32[]{:S(2)}) copy-start(f32[2,256,256]{2,1,0:T(8,128)} %param.7) | copy-start | bytes 1572868
  212.8 336.7 %all-reduce.5.cloned.1.call-start = ((), (), s32[]{:S(2)}) async-start(), calls=%async_computation.3 | async-start | bytes 1048576 | tf_op jit(solution)/shard_map/psum | solution.py:57
Sparse Core Ops, SparseCore 0:
  10.4 54.7 all-gather.1
  67.6 116.6 all-reduce.2
  213.0 79.0 reduce-scatter.3
  298.0 251.5 all-reduce.4
where the time goes:
time: 559 us; the launch traced here: 558 us
  waiting for transfers between devices  503 us (90%)
  matrix products  28 us (5%)
  between operations  13.9 us (2%)
  local copies, waits for them, and re-layouts  10.1 us (2%)
    psum x1, waiting for transfers between devices, per_device(): lax.psum(jnp.einsum('rkb,rkc->kbc', l_panel.reshape(l_panel.shape[0], 2,...  254 us
    psum x1, waiting for transfers between devices, broadcast(): return lax.psum(block, axis)  112 us
    unnamed x5, waiting for transfers between devices  79.7 us
    all_gather x1, waiting for transfers between devices, per_device(): row_panel = lax.all_gather(l_panel, 'pcol', axis=0, tiled=True)  57.2 us
    dot_general x1, matrix products, per_device(): jnp.dot(inverse_block, masked_cols, precision=lax.Precision.HIGHEST, pref...  25.4 us
  transfers between devices with their start and end apart: 4, of which 4 were waited for; matrix products, arithmetic and copies ran while one was open for 1% of the time, Pallas kernels for 0%

commit v1 on v0

v1 whole, which is shorter than its diff:
```python
import functools

import jax
import jax.numpy as jnp
from jax import lax
from jax.experimental import pallas as pl
from jax.experimental.pallas import tpu as pltpu
from jax.sharding import PartitionSpec as P

ROW, COL = "prow", "pcol"


def split(x):
    high = x.astype(jnp.bfloat16)
    low = (x - high.astype(jnp.float32)).astype(jnp.bfloat16)
    return high, low


def dot(a, b, contract):
    return lax.dot_general(a, b, ((contract, (0,)), ((), ())), preferred_element_type=jnp.float32)


def product_kernel(block, n_pieces, sets_ref, a_ref, mine_ref, other_ref, rows_ref, out_ref, z_ref, w_ref, t_ref):
    piece = mine_ref.shape[1]
    n_blocks = a_ref.shape[0] // block
    core = sets_ref[2 * n_blocks]
    column = sets_ref[2 * n_blocks + 1]
    for g, source in enumerate((mine_ref, other_ref)):
        for z in range(source.shape[0]):
            s = column ^ (2 * z + (core ^ g))
            z_ref[pl.ds(pl.multiple_of(s * piece, 16), piece), :] = source[z]
    for b in range(n_blocks):
        of_second = sets_ref[n_blocks + b].astype(jnp.float32)
        rows = pl.ds(b * block, block)
        z = z_ref[rows, :]
        for k, keep in enumerate((1.0 - of_second, of_second)):
            high, low = split(z * keep)
            w_ref[k, 0, rows, :] = high
            w_ref[k, 1, rows, :] = low
    t_ref[...] = jnp.zeros_like(t_ref)
    for b in range(n_blocks):
        k = sets_ref[b]
        rows = pl.ds(b * block, block)
        a_high, a_low = split(a_ref[rows, :])
        w_high = w_ref[k, 0]
        y = -(dot(a_high, w_high, (1,)) + dot(a_low, w_high, (1,)) + dot(a_high, w_ref[k, 1], (1,)))
        z_ref[rows, :] = y
        y_high, y_low = split(y)
        p_high, p_low = split(rows_ref[rows, :])
        t_ref[k] += dot(p_high, y_high, (0,)) + dot(p_low, y_high, (0,)) + dot(p_high, y_low, (0,))
    per = t_ref.shape[0] * block // n_pieces
    each = block // per
    for s in range(n_pieces):
        out_ref[s, :piece, :] = z_ref[s * piece : (s + 1) * piece, :]
        out_ref[s, piece:, :] = t_ref[s // each, (s % each) * per : (s % each + 1) * per, :]


def per_device(inverse_block, l_panel, d_inverse, owner_map, ancestors):
    block = d_inverse.shape[1]
    rows_dev = l_panel.shape[0]
    n_row = lax.axis_size(ROW)
    n_col = lax.axis_size(COL)
    row = lax.axis_index(ROW)
    col = lax.axis_index(COL)
    core = row % 2
    edge = inverse_block.shape[0]
    n_blocks = edge // block

    second = jnp.any(owner_map[:, None] == ancestors[1][None, :], axis=1).astype(jnp.int32)
    start = (row * n_col + col) * rows_dev
    row_blocks = (start + jnp.arange(rows_dev, dtype=jnp.int32)) // block
    row_second = jnp.any(
        (row_blocks[:, None] == jnp.arange(second.shape[0], dtype=jnp.int32)[None, :]) & (second[None, :] == 1),
        axis=1,
        keepdims=True,
    )
    z = jnp.where(row_second, l_panel[:, block:], l_panel[:, :block])

    z_rows = lax.all_gather(z, COL, axis=0, tiled=True)
    turned = lax.ppermute(
        z, (ROW, COL), [(j * n_col + s, (j ^ s) * n_col + j) for j in range(n_row) for s in range(n_col)]
    )
    groups = [list(range(c, n_row, 2)) for c in range(2)]
    mine = lax.all_gather(turned, ROW, axis=0, axis_index_groups=groups)
    other = lax.ppermute(mine, ROW, [(i, i ^ 1) for i in range(n_row)])

    sets = jnp.concatenate(
        [
            lax.dynamic_slice(second, (row * n_blocks,), (n_blocks,)),
            lax.dynamic_slice(second, (col * n_blocks,), (n_blocks,)),
            jnp.stack([core, col]).astype(jnp.int32),
        ]
    )
    per = 2 * block // n_col
    vmem = pl.BlockSpec(memory_space=pltpu.VMEM)
    sent = pl.pallas_call(
        functools.partial(product_kernel, block, n_col),
        out_shape=jax.ShapeDtypeStruct((n_col, rows_dev + per, block), jnp.float32),
        in_specs=[pl.BlockSpec(memory_space=pltpu.SMEM), vmem, vmem, vmem, vmem],
        out_specs=vmem,
        scratch_shapes=[
            pltpu.VMEM((edge, block), jnp.float32),
            pltpu.VMEM((2, 2, edge, block), jnp.bfloat16),
            pltpu.VMEM((2, block, block), jnp.float32),
        ],
        compiler_params=pltpu.CompilerParams(vmem_limit_bytes=40 * 1024 * 1024),
        cost_estimate=pl.CostEstimate(
            flops=6 * edge * edge * block, bytes_accessed=4 * edge * (edge + 4 * block), transcendentals=0
        ),
    )(sets, inverse_block, mine, other, z_rows)
    summed = jnp.sum(lax.all_to_all(sent, COL, 0, 0), axis=0)

    y = summed[:rows_dev]
    column = jnp.concatenate([jnp.where(row_second, 0.0, y), jnp.where(row_second, y, 0.0)], axis=1)

    half = per // 2
    low, high = summed[rows_dev : rows_dev + half], summed[rows_dev + half :]
    first = core == 0
    terms = jnp.where(first, low, high) + lax.ppermute(
        jnp.where(first, high, low), ROW, [(i, i ^ 1) for i in range(n_row)]
    )
    step = 2
    while step < n_row:
        terms = terms + lax.ppermute(terms, ROW, [(i, i ^ step) for i in range(n_row)])
        step *= 2
    here = lax.all_to_all(jnp.broadcast_to(terms[None], (n_col, half, block)), COL, 0, 0)
    there = lax.ppermute(here, ROW, [(i, i ^ 1) for i in range(n_row)])
    all_terms = jnp.stack([jnp.where(first, here, there), jnp.where(first, there, here)], axis=1)
    return column, d_inverse - all_terms.reshape(2, block, block)


def solution(mesh):
    return jax.shard_map(
        per_device,
        mesh=mesh,
        in_specs=(P(ROW, COL), P((ROW, COL), None), P(), P(), P()),
        out_specs=(P((ROW, COL), None), P()),
        check_vma=False,
    )
```

time: 559 us -> 147 us (0.26)
  waiting for transfers between devices: 503 us -> 38.3 us
  blocking collectives: 0 us -> 43.1 us
  starting transfers between devices: 0.16 us -> 32.4 us
  matrix products: 28 us -> 0 us
  Pallas kernels: 0 us -> 9.16 us
    psum x2 -> x0, waiting for transfers between devices: 366 us -> none  [the longest x1 254 us: per_device(): lax.psum(jnp.einsum('rkb,rkc->kbc', l_panel.reshape(l_panel.shape[0], 2,...]
    unnamed x5 -> x1, waiting for transfers between devices: 79.7 us -> 0.02 us
    all_gather x1, waiting for transfers between devices: 57.2 us -> 5.06 us  [per_device(): z_rows = lax.all_gather(z, COL, axis=0, tiled=True)]
    all_gather x0 -> x1, blocking collectives: none -> 33 us  [per_device(): mine = lax.all_gather(turned, ROW, axis=0, axis_index_groups=groups)]
    dot_general x4 -> x0, matrix products: 28 us -> none  [the longest x1 25.4 us: per_device(): jnp.dot(inverse_block, masked_cols, precision=lax.Precision.HIGHEST, pref...]
    ppermute x0 -> x7, starting transfers between devices: none -> 27.7 us  [the longest x3 9 us: per_device(): lax.ppermute(terms, ROW, [(i, i ^ step) for i in range(n_row)])]
    all_to_all x0 -> x1, waiting for transfers between devices: none -> 23.9 us  [per_device(): summed = jnp.sum(lax.all_to_all(sent, COL, 0, 0), axis=0)]
    all_to_all x0 -> x1, blocking collectives: none -> 10.1 us  [per_device(): lax.all_to_all(jnp.broadcast_to(terms[None], (n_col, half, block)), COL,...]
  transfers between devices with their start and end apart: 4 -> 9, of which waited for: 4 -> 9; matrix products, arithmetic and copies ran while one was open for 1% -> 1% of each run, Pallas kernels for 0% -> 0%
where the time goes in v1:
time: 147 us
  blocking collectives  43.1 us (29%)
  waiting for transfers between devices  38.3 us (26%)
  starting transfers between devices  32.4 us (22%)
  between operations  14.1 us (10%)
  Pallas kernels  9.16 us (6%)
  local copies, waits for them, and re-layouts  4.96 us (3%)
  other arithmetic  4.5 us (3%)
    all_gather x1, blocking collectives, per_device(): mine = lax.all_gather(turned, ROW, axis=0, axis_index_groups=groups)  33 us
    all_to_all x1, waiting for transfers between devices, per_device(): summed = jnp.sum(lax.all_to_all(sent, COL, 0, 0), axis=0)  23.9 us
    all_to_all x1, blocking collectives, per_device(): lax.all_to_all(jnp.broadcast_to(terms[None], (n_col, half, block)), COL,...  10.1 us
    pallas_call x1, Pallas kernels, per_device(): pl.pallas_call(functools.partial(product_kernel, block, n_col), out_shape...  9.16 us
    ppermute x3, starting transfers between devices, per_device(): lax.ppermute(terms, ROW, [(i, i ^ step) for i in range(n_row)])  9 us
    ppermute x1, starting transfers between devices, per_device(): other = lax.ppermute(mine, ROW, [(i, i ^ 1) for i in range(n_row)])  5.23 us
    all_gather x1, waiting for transfers between devices, per_device(): z_rows = lax.all_gather(z, COL, axis=0, tiled=True)  5.06 us
    ppermute x1, starting transfers between devices, per_device(): there = lax.ppermute(here, ROW, [(i, i ^ 1) for i in range(n_row)])  5.04 us
  transfers between devices with their start and end apart: 9, of which 9 were waited for; matrix products, arithmetic and copies ran while one was open for 1% of the time, Pallas kernels for 0%

profile of v1, /device:TPU:1, one launch (start us, length us, event | category | flops | bytes accessed | tf_op | source)
XLA Modules:
  0.0 146.7 jit_solution(13416454551964395303)
XLA Ops:
  7.2 0.0 all-gather.3.cloned.1.call-start
  7.2 0.7 slice_bitcast_fusion
  7.9 0.7 compare_reduce_fusion
  8.7 0.2 fusion.1
  8.9 1.6 %slice_select_fusion = f32[80,256]{1,0:T(8,128)} fusion(f32[80,512]{1,0:T(8,128)} %param.6, pred[80]{0:T(512)(128)(4,1)S(1)} %fusion.1), kind=kLoop, calls=%fused_computation.4 | loop fusion | flops 20480 | bytes 245840 | tf_op jit(solution)/shard_map/jit(_where)/select_n | solution.py:77
  10.5 0.0 all-gather.3.cloned.1.call-update
  10.5 3.9 %collective-permute-start = (f32[80,256]{1,0:T(8,128)}, f32[80,256]{1,0:T(8,128)S(1)}, u32[]{:S(2)}, u32[]{:S(2)}) collective-permute-start(f32[80,256]{1,0:T(8,128)} %slice_select_fusion), channel_id=1, source_target_pairs={{0,0},{1,16},{2,32},{3,48},{4,64},{5,80},{6,96},{7,112},{8,128},{9... | collective-permute-start | bytes 245768 | tf_op jit(solution)/shard_map/ppermute | solution.py:80
  14.5 2.9 %collective-permute-done = f32[80,256]{1,0:T(8,128)S(1)} collective-permute-done((f32[80,256]{1,0:T(8,128)}, f32[80,256]{1,0:T(8,128)S(1)}, u32[]{:S(2)}, u32[]{:S(2)}) %collective-permute-start) | collective-permute-done | bytes 81952 | tf_op jit(solution)/shard_map/ppermute | solution.py:80
  17.4 33.0 %all-gather = f32[640,256]{1,0:T(8,128)S(1)} all-gather(f32[80,256]{1,0:T(8,128)S(1)} %collective-permute-done), channel_id=2, replica_groups={{0,32,64,96,128,160,192,224},{16,48,80,112,144,176,208,240},{1,33,65,97..., dimensions={0}, use_global_device_ids=true | all-gather | bytes 737280 | tf_op jit(solution)/shard_map/all_gather | solution.py:84
  50.4 5.2 %collective-permute-start.1 = (f32[8,80,256]{2,1,0:T(8,128)S(1)}, f32[8,80,256]{2,1,0:T(8,128)S(1)}, u32[]{:S(2)}, u32[]{:S(2)}) collective-permute-start(f32[8,80,256]{2,1,0:T(8,128)S(1)} %bitcast.12), channel_id=1, source_target_pairs={{0,16},{16,0},{32,48},{48,32},{64,80},{80,64},{96,112},{112,96},{1... | collective-permute-start | bytes 1966088 | tf_op jit(solution)/shard_map/ppermute | solution.py:85
  55.6 0.1 fusion.2
  55.7 0.1 pad_add_fusion.sets_ref
  55.7 1.6 %collective-permute-done.1.other_ref = f32[8,80,256]{2,1,0:T(8,128)S(1)} collective-permute-done((f32[8,80,256]{2,1,0:T(8,128)S(1)}, f32[8,80,256]{2,1,0:T(8,128)S(1)}, u32[]{:S(2)}, u32[]{:S(2)}) %collective-permute-start.1) | collective-permute-done | bytes 655392 | tf_op jit(solution)/shard_map/ppermute | solution.py:85
  57.3 5.1 %all-gather.3.cloned.1.call-done.rows_ref = f32[1280,256]{1,0:T(8,128)} async-done(((f32[80,256]{1,0:T(8,128)}), f32[1280,256]{1,0:T(8,128)}) %all-gather.3.cloned.1.call-update) | async-done | bytes 1310736 | tf_op jit(solution)/shard_map/all_gather | solution.py:79
  62.4 0.0 copy-start
  62.4 2.9 %copy-done = f32[1280,1280]{1,0:T(8,128)S(1)} copy-done((f32[1280,1280]{1,0:T(8,128)S(1)}, f32[1280,1280]{1,0:T(8,128)}, u32[]{:S(2)}) %copy-start) | copy-done | bytes 6553624
  65.2 0.0 copy-start.1
  65.2 1.3 copy-done.1
  66.5 9.2 %shard_map.68 = f32[16,112,256]{2,1,0:T(8,128)} custom-call(s32[12]{0:T(128)S(1)} %pad_add_fusion.sets_ref, f32[1280,1280]{1,0:T(8,128)S(1)} %copy-done, f32[8,80,256]{2,1,0:T(8,128)S(1)} %bitcast.13, f32[8,80,256]{2,1,0:T(8,128)S(1)} %collective-permute-done.1.other_ref, f32[1280,256]{1,0:T(8,128)S(1)} %copy-done.1), custom_call_target="tpu_custom_call" | custom-call | flops 2516582400 | bytes 11796480 | tf_op jit(solution)/shard_map/pallas_call | solution.py:96
  75.7 4.7 %all-to-all-start = ((f32[16,112,256]{2,1,0:T(8,128)}), f32[16,112,256]{2,1,0:T(8,128)S(1)}, u32[]{:S(2)}, u32[]{:S(2)}) async-start(f32[16,112,256]{2,1,0:T(8,128)} %shard_map.68), calls=%async_computation | async-start | bytes 3670016 | tf_op jit(solution)/shard_map/all_to_all | solution.py:111
  80.4 23.9 %all-to-all-done = f32[16,112,256]{2,1,0:T(8,128)S(1)} async-done(((f32[16,112,256]{2,1,0:T(8,128)}), f32[16,112,256]{2,1,0:T(8,128)S(1)}, u32[]{:S(2)}, u32[]{:S(2)}) %all-to-all-start) | async-done | bytes 1835040 | tf_op jit(solution)/shard_map/all_to_all | solution.py:111
  104.3 0.1 reduce_sum.9
  104.4 0.0 copy-start.2
  104.4 4.5 %collective-permute-start.2 = (f32[16,256]{1,0:T(8,128)S(1)}, f32[16,256]{1,0:T(8,128)S(1)}, u32[]{:S(2)}, u32[]{:S(2)}) collective-permute-start(f32[16,256]{1,0:T(8,128)S(1)} %slice_select_fusion.3), channel_id=1, source_target_pairs={{0,16},{16,0},{32,48},{48,32},{64,80},{80,64},{96,112},{112,96},{1... | collective-permute-start | bytes 49160 | tf_op jit(solution)/shard_map/ppermute | solution.py:119
  108.9 0.8 collective-permute-done.2
  109.8 1.3 collective-permute-start.3
  111.1 1.3 collective-permute-done.3
  112.4 2.2 %collective-permute-start.4 = (f32[16,256]{1,0:T(8,128)S(1)}, f32[16,256]{1,0:T(8,128)S(1)}, u32[]{:S(2)}, u32[]{:S(2)}) collective-permute-start(f32[16,256]{1,0:T(8,128)S(1)} %add.47), channel_id=1, source_target_pairs={{0,64},{16,80},{32,96},{48,112},{64,0},{80,16},{96,32},{112,48},{1... | collective-permute-start | bytes 49160 | tf_op jit(solution)/shard_map/ppermute | solution.py:124
  114.6 1.2 collective-permute-done.4
  115.9 5.5 %collective-permute-start.5 = (f32[16,256]{1,0:T(8,128)S(1)}, f32[16,256]{1,0:T(8,128)S(1)}, u32[]{:S(2)}, u32[]{:S(2)}) collective-permute-start(f32[16,256]{1,0:T(8,128)S(1)} %add.48), channel_id=1, source_target_pairs={{0,128},{16,144},{32,160},{48,176},{64,192},{80,208},{96,224},{112... | collective-permute-start | bytes 49160 | tf_op jit(solution)/shard_map/ppermute | solution.py:124
  121.3 1.1 collective-permute-done.5
  122.5 10.1 %all_to_all.10 = f32[16,16,256]{2,1,0:T(8,128)S(1)} all-to-all(f32[16,16,256]{2,1,0:T(8,128)S(1)} %broadcast_in_dim.30), channel_id=1, replica_groups=mesh['prow'=16,'pcol'=16] {'pcol'}, dimensions={0} | all-to-all | bytes 524288 | tf_op jit(solution)/shard_map/all_to_all | solution.py:126
  132.6 5.0 %collective-permute-start.6 = (f32[16,16,256]{2,1,0:T(8,128)S(1)}, f32[16,16,256]{2,1,0:T(8,128)S(1)}, u32[]{:S(2)}, u32[]{:S(2)}) collective-permute-start(f32[16,16,256]{2,1,0:T(8,128)S(1)} %all_to_all.10), channel_id=1, source_target_pairs={{0,16},{16,0},{32,48},{48,32},{64,80},{80,64},{96,112},{112,96},{1... | collective-permute-start | bytes 786440 | tf_op jit(solution)/shard_map/ppermute | solution.py:127
  137.7 0.1 slice_select_fusion.2
  137.8 0.7 pad_maximum_fusion.1
  138.4 0.4 collective-permute-done.6
  138.9 0.0 copy-done.2
  138.9 0.9 sub.10
  (10 shorter events, 0.1 us)
Async XLA Ops:
  7.2 55.2 %all-gather.3.cloned.1.call-start = ((), (), s32[]{:S(2)}) async-start(), calls=%async_computation.2 | async-start | bytes 1392640 | tf_op jit(solution)/shard_map/all_gather | solution.py:79
  10.5 6.8 %collective-permute-start = (f32[80,256]{1,0:T(8,128)}, f32[80,256]{1,0:T(8,128)S(1)}, u32[]{:S(2)}, u32[]{:S(2)}) collective-permute-start(f32[80,256]{1,0:T(8,128)} %slice_select_fusion), channel_id=1, source_target_pairs={{0,0},{1,16},{2,32},{3,48},{4,64},{5,80},{6,96},{7,112},{8,128},{9... | collective-permute-start | bytes 245768 | tf_op jit(solution)/shard_map/ppermute | solution.py:80
  50.4 7.0 %collective-permute-start.1 = (f32[8,80,256]{2,1,0:T(8,128)S(1)}, f32[8,80,256]{2,1,0:T(8,128)S(1)}, u32[]{:S(2)}, u32[]{:S(2)}) collective-permute-start(f32[8,80,256]{2,1,0:T(8,128)S(1)} %bitcast.12), channel_id=1, source_target_pairs={{0,16},{16,0},{32,48},{48,32},{64,80},{80,64},{96,112},{112,96},{1... | collective-permute-start | bytes 1966088 | tf_op jit(solution)/shard_map/ppermute | solution.py:85
  62.4 2.9 %copy-start = (f32[1280,1280]{1,0:T(8,128)S(1)}, f32[1280,1280]{1,0:T(8,128)}, u32[]{:S(2)}) copy-start(f32[1280,1280]{1,0:T(8,128)} %a_ref.1) | copy-start | bytes 19660804
  65.2 1.3 copy-start.1
  75.7 28.6 %all-to-all-start = ((f32[16,112,256]{2,1,0:T(8,128)}), f32[16,112,256]{2,1,0:T(8,128)S(1)}, u32[]{:S(2)}, u32[]{:S(2)}) async-start(f32[16,112,256]{2,1,0:T(8,128)} %shard_map.68), calls=%async_computation | async-start | bytes 3670016 | tf_op jit(solution)/shard_map/all_to_all | solution.py:111
  104.4 34.5 %copy-start.2 = (f32[2,256,256]{2,1,0:T(8,128)S(1)}, f32[2,256,256]{2,1,0:T(8,128)}, u32[]{:S(2)}) copy-start(f32[2,256,256]{2,1,0:T(8,128)} %param.7) | copy-start | bytes 1572868
  104.4 5.4 %collective-permute-start.2 = (f32[16,256]{1,0:T(8,128)S(1)}, f32[16,256]{1,0:T(8,128)S(1)}, u32[]{:S(2)}, u32[]{:S(2)}) collective-permute-start(f32[16,256]{1,0:T(8,128)S(1)} %slice_select_fusion.3), channel_id=1, source_target_pairs={{0,16},{16,0},{32,48},{48,32},{64,80},{80,64},{96,112},{112,96},{1... | collective-permute-start | bytes 49160 | tf_op jit(solution)/shard_map/ppermute | solution.py:119
  109.8 2.6 %collective-permute-start.3 = (f32[16,256]{1,0:T(8,128)S(1)}, f32[16,256]{1,0:T(8,128)S(1)}, u32[]{:S(2)}, u32[]{:S(2)}) collective-permute-start(f32[16,256]{1,0:T(8,128)S(1)} %select_add_fusion), channel_id=1, source_target_pairs={{0,32},{16,48},{32,0},{48,16},{64,96},{80,112},{96,64},{112,80},{1... | collective-permute-start | bytes 49160 | tf_op jit(solution)/shard_map/ppermute | solution.py:124
  112.4 3.5 %collective-permute-start.4 = (f32[16,256]{1,0:T(8,128)S(1)}, f32[16,256]{1,0:T(8,128)S(1)}, u32[]{:S(2)}, u32[]{:S(2)}) collective-permute-start(f32[16,256]{1,0:T(8,128)S(1)} %add.47), channel_id=1, source_target_pairs={{0,64},{16,80},{32,96},{48,112},{64,0},{80,16},{96,32},{112,48},{1... | collective-permute-start | bytes 49160 | tf_op jit(solution)/shard_map/ppermute | solution.py:124
  115.9 6.6 %collective-permute-start.5 = (f32[16,256]{1,0:T(8,128)S(1)}, f32[16,256]{1,0:T(8,128)S(1)}, u32[]{:S(2)}, u32[]{:S(2)}) collective-permute-start(f32[16,256]{1,0:T(8,128)S(1)} %add.48), channel_id=1, source_target_pairs={{0,128},{16,144},{32,160},{48,176},{64,192},{80,208},{96,224},{112... | collective-permute-start | bytes 49160 | tf_op jit(solution)/shard_map/ppermute | solution.py:124
  132.6 6.2 %collective-permute-start.6 = (f32[16,16,256]{2,1,0:T(8,128)S(1)}, f32[16,16,256]{2,1,0:T(8,128)S(1)}, u32[]{:S(2)}, u32[]{:S(2)}) collective-permute-start(f32[16,16,256]{2,1,0:T(8,128)S(1)} %all_to_all.10), channel_id=1, source_target_pairs={{0,16},{16,0},{32,48},{48,32},{64,80},{80,64},{96,112},{112,96},{1... | collective-permute-start | bytes 786440 | tf_op jit(solution)/shard_map/ppermute | solution.py:127
Sparse Core Ops, SparseCore 0:
  11.0 51.3 all-gather.2

commit v2 on v1

v2 whole, which is shorter than its diff:
```python
import functools

import jax
import jax.numpy as jnp
from jax import lax
from jax.experimental import pallas as pl
from jax.experimental.pallas import tpu as pltpu
from jax.sharding import PartitionSpec as P

ROW, COL = "prow", "pcol"


def split(x):
    high = x.astype(jnp.bfloat16)
    low = (x - high.astype(jnp.float32)).astype(jnp.bfloat16)
    return high, low


def dot(a, b, contract):
    return lax.dot_general(a, b, ((contract, (0,)), ((), ())), preferred_element_type=jnp.float32)


def dot3(a, b, contract):
    (a_high, a_low), (b_high, b_low) = a, b
    return dot(a_high, b_high, contract) + dot(a_low, b_high, contract) + dot(a_high, b_low, contract)


def in_second(owner_ref, ancestors_ref, stored):
    number = owner_ref[stored]
    found = jnp.int32(0)
    for a in range(ancestors_ref.shape[1]):
        found = found | (ancestors_ref[1, a] == number).astype(jnp.int32)
    return found


def second_rows(block, n_col, owner_ref, ancestors_ref, shape):
    start = (lax.axis_index(ROW) * n_col + lax.axis_index(COL)) * shape[0]
    first = start // block
    last = (start + shape[0] - 1) // block
    here = start + lax.broadcasted_iota(jnp.int32, shape, 0)
    in_first = in_second(owner_ref, ancestors_ref, first)
    in_last = in_second(owner_ref, ancestors_ref, last)
    return jnp.where(here < (first + 1) * block, in_first, in_last) == 1


def pick_kernel(block, n_col, owner_ref, ancestors_ref, panel_ref, z_ref):
    second = second_rows(block, n_col, owner_ref, ancestors_ref, z_ref.shape)
    z_ref[...] = jnp.where(second, panel_ref[:, block:], panel_ref[:, :block])


def split_kernel(owner_ref, ancestors_ref, a_ref, high_ref, low_ref, sets_ref):
    n = pl.num_programs(0)
    b = pl.program_id(0)
    sets_ref[b] = in_second(owner_ref, ancestors_ref, lax.axis_index(ROW) * n + b)
    sets_ref[n + b] = in_second(owner_ref, ancestors_ref, lax.axis_index(COL) * n + b)
    high_ref[...], low_ref[...] = split(a_ref[...])


def product_kernel(block, sets_ref, high_ref, low_ref, *refs):
    *sources, out_ref, z_ref, w_ref = refs
    piece = out_ref.shape[1]
    n_blocks = high_ref.shape[0] // block
    n_z = out_ref.shape[0] // 2
    row = lax.axis_index(ROW)
    core = row % 2
    column = lax.axis_index(COL)
    steps = [0, 1, 2, 3, 4, 1, 2, 3, 4]
    for n, (source, step) in enumerate(zip(sources, steps)):
        owner = core if n < 5 else 1 - core
        z = (row // 2 + n_z + step * (2 * owner - 1)) % n_z
        for h in range(source.shape[0] // piece):
            s = column ^ (2 * z + (owner ^ h))
            z_ref[pl.ds(pl.multiple_of(s * piece, 16), piece), :] = source[h * piece : (h + 1) * piece, :]
    for b in range(n_blocks):
        of_second = sets_ref[n_blocks + b].astype(jnp.float32)
        rows = pl.ds(b * block, block)
        z = z_ref[rows, :]
        for k, keep in enumerate((1.0 - of_second, of_second)):
            w_ref[k, 0, rows, :], w_ref[k, 1, rows, :] = split(z * keep)
    for b in range(n_blocks):
        k = sets_ref[b]
        rows = pl.ds(b * block, block)
        z_ref[rows, :] = -dot3((high_ref[rows, :], low_ref[rows, :]), (w_ref[k, 0], w_ref[k, 1]), (1,))
    for s in range(out_ref.shape[0]):
        out_ref[s] = z_ref[s * piece : (s + 1) * piece, :]


def finish_kernel(block, n_col, owner_ref, ancestors_ref, parts_ref, z_ref, column_ref, keep_ref, send_ref):
    y = parts_ref[0]
    for s in range(1, parts_ref.shape[0]):
        y = y + parts_ref[s]
    second = second_rows(block, n_col, owner_ref, ancestors_ref, y.shape)
    column_ref[:, :block] = jnp.where(second, 0.0, y)
    column_ref[:, block:] = jnp.where(second, y, 0.0)
    z = z_ref[...]
    kept = second == (lax.axis_index(ROW) % 2 == 1)
    y = split(y)
    keep_ref[...] = dot3(split(jnp.where(kept, z, 0.0)), y, (0,))
    send_ref[...] = dot3(split(jnp.where(kept, 0.0, z)), y, (0,))


def per_device(inverse_block, l_panel, d_inverse, owner_map, ancestors):
    block = d_inverse.shape[1]
    rows_dev = l_panel.shape[0]
    n_row = lax.axis_size(ROW)
    n_col = lax.axis_size(COL)
    edge = inverse_block.shape[0]
    n_blocks = edge // block
    n_z = n_row // 2
    f32 = jnp.float32
    smem = pl.BlockSpec(memory_space=pltpu.SMEM)
    vmem = pl.BlockSpec(memory_space=pltpu.VMEM)
    limit = lambda mib: mib * 1024 * 1024
    swap = [(i, i ^ 1) for i in range(n_row)]
    groups = [list(range(c, n_row, 2)) for c in range(2)]

    z = pl.pallas_call(
        functools.partial(pick_kernel, block, n_col),
        out_shape=jax.ShapeDtypeStruct((rows_dev, block), f32),
        in_specs=[smem, smem, vmem],
        out_specs=vmem,
        compiler_params=pltpu.CompilerParams(vmem_limit_bytes=limit(4)),
    )(owner_map, ancestors, l_panel)
    turned = lax.ppermute(
        z, (ROW, COL), [(j * n_col + s, (j ^ s) * n_col + j) for j in range(n_row) for s in range(n_col)]
    )
    strip = pl.BlockSpec((block, edge), lambda b: (b, 0))
    high, low, sets = pl.pallas_call(
        split_kernel,
        grid=(n_blocks,),
        out_shape=[
            jax.ShapeDtypeStruct((edge, edge), jnp.bfloat16),
            jax.ShapeDtypeStruct((edge, edge), jnp.bfloat16),
            jax.ShapeDtypeStruct((2 * n_blocks,), jnp.int32),
        ],
        in_specs=[smem, smem, strip],
        out_specs=[strip, strip, smem],
        compiler_params=pltpu.CompilerParams(vmem_limit_bytes=limit(16)),
        cost_estimate=pl.CostEstimate(flops=4 * edge * edge, bytes_accessed=8 * edge * edge, transcendentals=0),
    )(owner_map, ancestors, inverse_block)
    turned, high, low, sets = lax.optimization_barrier((turned, high, low, sets))

    def along(x, step):
        pairs = [(2 * q + c, 2 * ((q + step * (1 - 2 * c)) % n_z) + c) for q in range(n_z) for c in range(2)]
        return lax.ppermute(x, ROW, pairs)

    chunk = jnp.concatenate([turned, lax.ppermute(turned, ROW, swap)])
    one, two = along(chunk, 1), along(chunk, 2)
    three, four = along(two, 1), along(two[:rows_dev], 2)
    pieces = [one, two, three, four]
    pieces = [chunk, *pieces, *(lax.ppermute(p, ROW, swap) for p in pieces)]

    sent = pl.pallas_call(
        functools.partial(product_kernel, block),
        out_shape=jax.ShapeDtypeStruct((n_col, rows_dev, block), f32),
        in_specs=[smem, vmem, vmem] + [vmem] * len(pieces),
        out_specs=vmem,
        scratch_shapes=[pltpu.VMEM((edge, block), f32), pltpu.VMEM((2, 2, edge, block), jnp.bfloat16)],
        compiler_params=pltpu.CompilerParams(vmem_limit_bytes=limit(20)),
        cost_estimate=pl.CostEstimate(
            flops=6 * edge * edge * block, bytes_accessed=4 * edge * (edge + 2 * block), transcendentals=0
        ),
    )(sets, high, low, *pieces)
    parts = lax.all_to_all(sent, COL, 0, 0)

    column, keep, send = pl.pallas_call(
        functools.partial(finish_kernel, block, n_col),
        out_shape=[
            jax.ShapeDtypeStruct((rows_dev, 2 * block), f32),
            jax.ShapeDtypeStruct((block, block), f32),
            jax.ShapeDtypeStruct((block, block), f32),
        ],
        in_specs=[smem, smem, vmem, vmem],
        out_specs=[vmem, vmem, vmem],
        compiler_params=pltpu.CompilerParams(vmem_limit_bytes=limit(12)),
    )(owner_map, ancestors, parts, z)

    per = block // n_col
    terms = keep + lax.ppermute(send, ROW, swap)
    terms = jnp.sum(lax.all_to_all(terms.reshape(n_col, per, block), COL, 0, 0), axis=0)
    terms = jnp.broadcast_to(terms[None], (n_z, per, block))
    terms = jnp.sum(lax.all_to_all(terms, ROW, 0, 0, axis_index_groups=groups), axis=0)
    terms = jnp.broadcast_to(terms[None], (n_col, per, block))
    here = lax.all_to_all(terms, COL, 0, 0).reshape(block, block)
    there = lax.ppermute(here, ROW, swap)
    first = lax.axis_index(ROW) % 2 == 0
    diag = d_inverse - jnp.stack([jnp.where(first, here, there), jnp.where(first, there, here)])
    return column, diag


def solution(mesh):
    return jax.shard_map(
        per_device,
        mesh=mesh,
        in_specs=(P(ROW, COL), P((ROW, COL), None), P(), P(), P()),
        out_specs=(P((ROW, COL), None), P()),
        check_vma=False,
    )
```

time: 147 us -> 114 us (0.78)
  waiting for transfers between devices: 38.3 us -> 6.81 us
  blocking collectives: 43.1 us -> 58.8 us
  between operations: 14.1 us -> 0.77 us
  other arithmetic: 4.5 us -> 0.97 us
  local copies, waits for them, and re-layouts: 4.96 us -> 6.49 us
    all_to_all x1 -> x4, blocking collectives: 10.1 us -> 58.8 us  [the longest x1 25 us: per_device(): parts = lax.all_to_all(sent, COL, 0, 0)]
    all_gather x1 -> x0, blocking collectives: 33 us -> none  [per_device(): mine = lax.all_gather(turned, ROW, axis=0, axis_index_groups=groups)]
    all_to_all x1 -> x0, waiting for transfers between devices: 23.9 us -> none  [per_device(): summed = jnp.sum(lax.all_to_all(sent, COL, 0, 0), axis=0)]
    all_gather x1 -> x0, waiting for transfers between devices: 5.06 us -> none  [per_device(): z_rows = lax.all_gather(z, COL, axis=0, tiled=True)]
    all_to_all x1 -> x0, starting transfers between devices: 4.66 us -> none  [per_device(): summed = jnp.sum(lax.all_to_all(sent, COL, 0, 0), axis=0)]
    ppermute x6 -> x11, starting transfers between devices: 23.8 us -> 28.1 us  [the longest x4 16.1 us: along(): return lax.ppermute(x, ROW, pairs)]
    ppermute x1, waiting for transfers between devices: 2.88 us -> 0.01 us  [per_device(): lax.ppermute(z, (ROW, COL), [(j * n_col + s, (j ^ s) * n_col + j) for j i...]
    unnamed x6 -> x19, local copies, waits for them, and re-layouts: 4.18 us -> 6.45 us
  transfers between devices with their start and end apart: 9 -> 12, of which waited for: 9 -> 5; matrix products, arithmetic and copies ran while one was open for 1% -> 0% of each run, Pallas kernels for 0% -> 2%
where the time goes in v2:
time: 114 us
  blocking collectives  58.8 us (52%)
  starting transfers between devices  32 us (28%)
  Pallas kernels  8.2 us (7%)
  waiting for transfers between devices  6.81 us (6%)
  local copies, waits for them, and re-layouts  6.49 us (6%)
    all_to_all x1, blocking collectives, per_device(): parts = lax.all_to_all(sent, COL, 0, 0)  25 us
    ppermute x4, starting transfers between devices, along(): return lax.ppermute(x, ROW, pairs)  16.1 us
    all_to_all x1, blocking collectives, per_device(): lax.all_to_all(terms, ROW, 0, 0, axis_index_groups=groups)  12.9 us
    all_to_all x1, blocking collectives, per_device(): lax.all_to_all(terms.reshape(n_col, per, block), COL, 0, 0)  10.7 us
    all_to_all x1, blocking collectives, per_device(): here = lax.all_to_all(terms, COL, 0, 0).reshape(block, block)  10.1 us
    unnamed x19, local copies, waits for them, and re-layouts  6.45 us
    ppermute x4, starting transfers between devices, per_device(): pieces = [chunk, *pieces, *(lax.ppermute(p, ROW, swap) for p in pieces)]  6.07 us
    ppermute x1, starting transfers between devices, per_device(): there = lax.ppermute(here, ROW, swap)  4.4 us
  transfers between devices with their start and end apart: 12, of which 5 were waited for; matrix products, arithmetic and copies ran while one was open for 0% of the time, Pallas kernels for 2%

profile of v2, /device:TPU:1, one launch (start us, length us, event | category | flops | bytes accessed | tf_op | source)
XLA Modules:
  0.0 114.1 jit_solution(5878342380131926022)
XLA Ops:
  0.6 0.0 copy-start.1
  0.6 0.9 copy-done.1
  1.5 0.0 copy-start.2
  1.5 0.7 copy-done.2
  2.2 0.0 copy-start.5
  2.2 0.7 copy-done.5
  2.9 0.6 shard_map.68.z_ref
  3.5 3.9 %collective-permute-start = (f32[80,256]{1,0:T(8,128)S(1)}, f32[80,256]{1,0:T(8,128)S(1)}, u32[]{:S(2)}, u32[]{:S(2)}) collective-permute-start(f32[80,256]{1,0:T(8,128)S(1)} %shard_map.68.z_ref), channel_id=1, source_target_pairs={{0,0},{1,16},{2,32},{3,48},{4,64},{5,80},{6,96},{7,112},{8,128},{9... | collective-permute-start | bytes 245768 | tf_op jit(solution)/shard_map/ppermute | solution.py:124
  7.5 0.0 copy-start
  7.5 2.9 %copy-done = f32[1280,1280]{1,0:T(8,128)S(1)} copy-done((f32[1280,1280]{1,0:T(8,128)S(1)}, f32[1280,1280]{1,0:T(8,128)}, u32[]{:S(2)}) %copy-start) | copy-done | bytes 6553624
  10.3 0.0 copy-start.3
  10.3 0.7 copy-done.3
  11.0 0.0 copy-start.6
  11.0 0.7 copy-done.6
  11.7 2.2 %shard_map.69 = (bf16[1280,1280]{1,0:T(8,128)(2,1)S(1)}, bf16[1280,1280]{1,0:T(8,128)(2,1)S(1)}, s32[10]{0:T(128)S(1)}) custom-call(s32[80]{0:T(128)S(1)} %copy-done.6, s32[2,40]{1,0:T(2,128)S(1)} %copy-done.3, f32[1280,1280]{1,0:T(8,128)S(1)} %copy-done), custom_call_target="tpu_custom_call" | custom-call | flops 6553600 | bytes 13107200 | tf_op jit(solution)/shard_map/pallas_call | solution.py:128
  13.9 0.0 collective-permute-done
  13.9 0.1 collective-permute-start.1
  14.0 1.2 %collective-permute-done.1 = f32[80,256]{1,0:T(8,128)S(1)} collective-permute-done((f32[80,256]{1,0:T(8,128)S(1)}, f32[80,256]{1,0:T(8,128)S(1)}, u32[]{:S(2)}, u32[]{:S(2)}) %collective-permute-start.1) | collective-permute-done | bytes 81952 | tf_op jit(solution)/shard_map/ppermute | solution.py:147
  15.3 10.0 %collective-permute-start.3 = (f32[160,256]{1,0:T(8,128)S(1)}, f32[160,256]{1,0:T(8,128)S(1)}, u32[]{:S(2)}, u32[]{:S(2)}) collective-permute-start(f32[160,256]{1,0:T(8,128)S(1)} %constant_dynamic-update-slice_fusion.refs_0_), channel_id=1, source_target_pairs={{0,64},{16,208},{32,96},{48,240},{64,128},{80,16},{96,160},{112,48... | collective-permute-start | bytes 491528 | tf_op jit(solution)/shard_map/ppermute | solution.py:145
  25.2 1.7 %collective-permute-start.2 = (f32[160,256]{1,0:T(8,128)S(1)}, f32[160,256]{1,0:T(8,128)S(1)}, u32[]{:S(2)}, u32[]{:S(2)}) collective-permute-start(f32[160,256]{1,0:T(8,128)S(1)} %constant_dynamic-update-slice_fusion.refs_0_), channel_id=1, source_target_pairs={{0,32},{16,240},{32,64},{48,16},{64,96},{80,48},{96,128},{112,80},... | collective-permute-start | bytes 491528 | tf_op jit(solution)/shard_map/ppermute | solution.py:145
  27.0 2.3 %collective-permute-done.3.refs_2_ = f32[160,256]{1,0:T(8,128)S(1)} collective-permute-done((f32[160,256]{1,0:T(8,128)S(1)}, f32[160,256]{1,0:T(8,128)S(1)}, u32[]{:S(2)}, u32[]{:S(2)}) %collective-permute-start.3) | collective-permute-done | bytes 163872 | tf_op jit(solution)/shard_map/ppermute | solution.py:145
  29.2 2.6 %collective-permute-start.4 = (f32[160,256]{1,0:T(8,128)S(1)}, f32[160,256]{1,0:T(8,128)S(1)}, u32[]{:S(2)}, u32[]{:S(2)}) collective-permute-start(f32[160,256]{1,0:T(8,128)S(1)} %collective-permute-done.3.refs_2_), channel_id=1, source_target_pairs={{0,32},{16,240},{32,64},{48,16},{64,96},{80,48},{96,128},{112,80},... | collective-permute-start | bytes 491528 | tf_op jit(solution)/shard_map/ppermute | solution.py:145
  31.8 0.0 copy-start.4
  31.8 0.0 copy-start.7
  31.8 1.8 %collective-permute-start.5 = (f32[80,256]{1,0:T(8,128)S(1)}, f32[80,256]{1,0:T(8,128)S(1)}, u32[]{:S(2)}, u32[]{:S(2)}) collective-permute-start(f32[80,256]{1,0:T(8,128)S(1)} %slice.4), channel_id=1, source_target_pairs={{0,64},{16,208},{32,96},{48,240},{64,128},{80,16},{96,160},{112,48... | collective-permute-start | bytes 245768 | tf_op jit(solution)/shard_map/ppermute | solution.py:145
  33.7 0.5 collective-permute-start.7
  34.1 0.0 collective-permute-done.2.refs_1_
  34.1 0.0 collective-permute-start.6
  34.2 0.0 collective-permute-done.4.refs_3_
  34.2 3.2 %collective-permute-start.8 = (f32[160,256]{1,0:T(8,128)S(1)}, f32[160,256]{1,0:T(8,128)S(1)}, u32[]{:S(2)}, u32[]{:S(2)}) collective-permute-start(f32[160,256]{1,0:T(8,128)S(1)} %collective-permute-done.4.refs_3_), channel_id=1, source_target_pairs={{0,16},{16,0},{32,48},{48,32},{64,80},{80,64},{96,112},{112,96},{1... | collective-permute-start | bytes 491528 | tf_op jit(solution)/shard_map/ppermute | solution.py:151
  37.4 0.0 collective-permute-done.5.refs_4_
  37.4 2.3 %collective-permute-start.9 = (f32[80,256]{1,0:T(8,128)S(1)}, f32[80,256]{1,0:T(8,128)S(1)}, u32[]{:S(2)}, u32[]{:S(2)}) collective-permute-start(f32[80,256]{1,0:T(8,128)S(1)} %collective-permute-done.5.refs_4_), channel_id=1, source_target_pairs={{0,16},{16,0},{32,48},{48,32},{64,80},{80,64},{96,112},{112,96},{1... | collective-permute-start | bytes 245768 | tf_op jit(solution)/shard_map/ppermute | solution.py:151
  39.7 0.9 collective-permute-done.9.refs_8_
  40.7 0.0 collective-permute-done.7.refs_6_
  40.7 0.0 collective-permute-done.6.refs_5_
  40.7 0.0 collective-permute-done.8.refs_7_
  40.7 4.0 %shard_map.70 = f32[16,80,256]{2,1,0:T(8,128)S(1)} custom-call(s32[10]{0:T(128)S(1)} %get-tuple-element.15.sets_ref, bf16[1280,1280]{1,0:T(8,128)(2,1)S(1)} %get-tuple-element.16.high_ref, bf16[1280,1280]{1,0:T(8,128)(2,1)S(1)} %get-tuple-element.17.low_ref, f32[160,256]{1,0:T(8,128)S(1)} %constant_dynamic-update-slice_fusion.refs_0_, ...), custom_call_target="tpu_custom_call" | custom-call | flops 2516582400 | bytes 9175040 | tf_op jit(solution)/shard_map/pallas_call | solution.py:153
  44.7 25.0 %all_to_all.20.parts_ref = f32[16,80,256]{2,1,0:T(8,128)S(1)} all-to-all(f32[16,80,256]{2,1,0:T(8,128)S(1)} %shard_map.70), channel_id=1, replica_groups=mesh['prow'=16,'pcol'=16] {'pcol'}, dimensions={0} | all-to-all | bytes 2621440 | tf_op jit(solution)/shard_map/all_to_all | solution.py:164
  69.7 0.0 copy-done.4
  69.7 0.0 copy-done.7
  69.7 0.0 copy-start.8
  69.7 1.3 %shard_map.71 = (f32[80,512]{1,0:T(8,128)}, f32[256,256]{1,0:T(8,128)S(1)}, f32[256,256]{1,0:T(8,128)S(1)}) custom-call(s32[80]{0:T(128)S(1)} %copy-done.7, s32[2,40]{1,0:T(2,128)S(1)} %copy-done.4, f32[16,80,256]{2,1,0:T(8,128)S(1)} %all_to_all.20.parts_ref, f32[80,256]{1,0:T(8,128)S(1)} %shard_map.68.z_ref), custom_call_target="tpu_custom_call" | custom-call | tf_op jit(solution)/shard_map/pallas_call | solution.py:166
  71.1 1.5 %collective-permute-start.10 = (f32[256,256]{1,0:T(8,128)S(1)}, f32[256,256]{1,0:T(8,128)S(1)}, u32[]{:S(2)}, u32[]{:S(2)}) collective-permute-start(f32[256,256]{1,0:T(8,128)S(1)} %get-tuple-element.21), channel_id=1, source_target_pairs={{0,16},{16,0},{32,48},{48,32},{64,80},{80,64},{96,112},{112,96},{1... | collective-permute-start | bytes 786440 | tf_op jit(solution)/shard_map/ppermute | solution.py:179
  72.5 1.2 %collective-permute-done.10 = f32[256,256]{1,0:T(8,128)S(1)} collective-permute-done((f32[256,256]{1,0:T(8,128)S(1)}, f32[256,256]{1,0:T(8,128)S(1)}, u32[]{:S(2)}, u32[]{:S(2)}) %collective-permute-start.10) | collective-permute-done | bytes 262176 | tf_op jit(solution)/shard_map/ppermute | solution.py:179
  73.7 10.7 %all_to_all.21 = f32[16,16,256]{2,1,0:T(8,128)S(1)} all-to-all(f32[16,16,256]{2,1,0:T(8,128)S(1)} %bitcast.8), channel_id=1, replica_groups=mesh['prow'=16,'pcol'=16] {'pcol'}, dimensions={0} | all-to-all | bytes 524288 | tf_op jit(solution)/shard_map/all_to_all | solution.py:180
  84.5 12.9 %all_to_all.22 = f32[8,16,256]{2,1,0:T(8,128)S(1)} all-to-all(f32[8,16,256]{2,1,0:T(8,128)S(1)} %broadcast_in_dim.4), channel_id=1, replica_groups={{0,32,64,96,128,160,192,224},{16,48,80,112,144,176,208,240},{1,33,65,97..., dimensions={0} | all-to-all | bytes 262144 | tf_op jit(solution)/shard_map/all_to_all | solution.py:182
  97.4 10.1 %all_to_all.23 = f32[16,16,256]{2,1,0:T(8,128)S(1)} all-to-all(f32[16,16,256]{2,1,0:T(8,128)S(1)} %broadcast_in_dim.5), channel_id=1, replica_groups=mesh['prow'=16,'pcol'=16] {'pcol'}, dimensions={0} | all-to-all | bytes 524288 | tf_op jit(solution)/shard_map/all_to_all | solution.py:184
  107.6 4.4 %collective-permute-start.11 = (f32[256,256]{1,0:T(8,128)S(1)}, f32[256,256]{1,0:T(8,128)S(1)}, u32[]{:S(2)}, u32[]{:S(2)}) collective-permute-start(f32[256,256]{1,0:T(8,128)S(1)} %bitcast.9), channel_id=1, source_target_pairs={{0,16},{16,0},{32,48},{48,32},{64,80},{80,64},{96,112},{112,96},{1... | collective-permute-start | bytes 786440 | tf_op jit(solution)/shard_map/ppermute | solution.py:185
  112.0 1.2 %collective-permute-done.11 = f32[256,256]{1,0:T(8,128)S(1)} collective-permute-done((f32[256,256]{1,0:T(8,128)S(1)}, f32[256,256]{1,0:T(8,128)S(1)}, u32[]{:S(2)}, u32[]{:S(2)}) %collective-permute-start.11) | collective-permute-done | bytes 262176 | tf_op jit(solution)/shard_map/ppermute | solution.py:185
  113.2 0.0 copy-done.8
  113.2 0.9 maximum_subtract_fusion
  (9 shorter events, 0.2 us)
Async XLA Ops:
  0.6 0.9 copy-start.1
  1.5 0.7 copy-start.2
  2.2 0.7 copy-start.5
  3.5 10.4 %collective-permute-start = (f32[80,256]{1,0:T(8,128)S(1)}, f32[80,256]{1,0:T(8,128)S(1)}, u32[]{:S(2)}, u32[]{:S(2)}) collective-permute-start(f32[80,256]{1,0:T(8,128)S(1)} %shard_map.68.z_ref), channel_id=1, source_target_pairs={{0,0},{1,16},{2,32},{3,48},{4,64},{5,80},{6,96},{7,112},{8,128},{9... | collective-permute-start | bytes 245768 | tf_op jit(solution)/shard_map/ppermute | solution.py:124
  7.5 2.9 %copy-start = (f32[1280,1280]{1,0:T(8,128)S(1)}, f32[1280,1280]{1,0:T(8,128)}, u32[]{:S(2)}) copy-start(f32[1280,1280]{1,0:T(8,128)} %a_ref.1) | copy-start | bytes 19660804
  10.3 0.7 copy-start.3
  11.0 0.7 copy-start.6
  13.9 1.4 %collective-permute-start.1 = (f32[80,256]{1,0:T(8,128)S(1)}, f32[80,256]{1,0:T(8,128)S(1)}, u32[]{:S(2)}, u32[]{:S(2)}) collective-permute-start(f32[80,256]{1,0:T(8,128)S(1)} %collective-permute-done), channel_id=1, source_target_pairs={{0,16},{16,0},{32,48},{48,32},{64,80},{80,64},{96,112},{112,96},{1... | collective-permute-start | bytes 245768 | tf_op jit(solution)/shard_map/ppermute | solution.py:147
  15.3 14.0 %collective-permute-start.3 = (f32[160,256]{1,0:T(8,128)S(1)}, f32[160,256]{1,0:T(8,128)S(1)}, u32[]{:S(2)}, u32[]{:S(2)}) collective-permute-start(f32[160,256]{1,0:T(8,128)S(1)} %constant_dynamic-update-slice_fusion.refs_0_), channel_id=1, source_target_pairs={{0,64},{16,208},{32,96},{48,240},{64,128},{80,16},{96,160},{112,48... | collective-permute-start | bytes 491528 | tf_op jit(solution)/shard_map/ppermute | solution.py:145
  25.2 8.9 %collective-permute-start.2 = (f32[160,256]{1,0:T(8,128)S(1)}, f32[160,256]{1,0:T(8,128)S(1)}, u32[]{:S(2)}, u32[]{:S(2)}) collective-permute-start(f32[160,256]{1,0:T(8,128)S(1)} %constant_dynamic-update-slice_fusion.refs_0_), channel_id=1, source_target_pairs={{0,32},{16,240},{32,64},{48,16},{64,96},{80,48},{96,128},{112,80},... | collective-permute-start | bytes 491528 | tf_op jit(solution)/shard_map/ppermute | solution.py:145
  29.2 4.9 %collective-permute-start.4 = (f32[160,256]{1,0:T(8,128)S(1)}, f32[160,256]{1,0:T(8,128)S(1)}, u32[]{:S(2)}, u32[]{:S(2)}) collective-permute-start(f32[160,256]{1,0:T(8,128)S(1)} %collective-permute-done.3.refs_2_), channel_id=1, source_target_pairs={{0,32},{16,240},{32,64},{48,16},{64,96},{80,48},{96,128},{112,80},... | collective-permute-start | bytes 491528 | tf_op jit(solution)/shard_map/ppermute | solution.py:145
  31.8 37.9 %copy-start.4 = (s32[2,40]{1,0:T(2,128)S(1)}, s32[2,40]{1,0:T(2,128)}, u32[]{:S(2)}) copy-start(s32[2,40]{1,0:T(2,128)} %ancestors_ref.5) | copy-start | bytes 964
  31.8 37.9 %copy-start.7 = (s32[80]{0:T(128)S(1)}, s32[80]{0:T(128)}, u32[]{:S(2)}) copy-start(s32[80]{0:T(128)} %owner_ref.5) | copy-start | bytes 964
  31.8 5.6 %collective-permute-start.5 = (f32[80,256]{1,0:T(8,128)S(1)}, f32[80,256]{1,0:T(8,128)S(1)}, u32[]{:S(2)}, u32[]{:S(2)}) collective-permute-start(f32[80,256]{1,0:T(8,128)S(1)} %slice.4), channel_id=1, source_target_pairs={{0,64},{16,208},{32,96},{48,240},{64,128},{80,16},{96,160},{112,48... | collective-permute-start | bytes 245768 | tf_op jit(solution)/shard_map/ppermute | solution.py:145
  33.7 7.0 %collective-permute-start.7 = (f32[160,256]{1,0:T(8,128)S(1)}, f32[160,256]{1,0:T(8,128)S(1)}, u32[]{:S(2)}, u32[]{:S(2)}) collective-permute-start(f32[160,256]{1,0:T(8,128)S(1)} %collective-permute-done.3.refs_2_), channel_id=1, source_target_pairs={{0,16},{16,0},{32,48},{48,32},{64,80},{80,64},{96,112},{112,96},{1... | collective-permute-start | bytes 491528 | tf_op jit(solution)/shard_map/ppermute | solution.py:151
  34.1 6.5 %collective-permute-start.6 = (f32[160,256]{1,0:T(8,128)S(1)}, f32[160,256]{1,0:T(8,128)S(1)}, u32[]{:S(2)}, u32[]{:S(2)}) collective-permute-start(f32[160,256]{1,0:T(8,128)S(1)} %collective-permute-done.2.refs_1_), channel_id=1, source_target_pairs={{0,16},{16,0},{32,48},{48,32},{64,80},{80,64},{96,112},{112,96},{1... | collective-permute-start | bytes 491528 | tf_op jit(solution)/shard_map/ppermute | solution.py:151
  34.2 6.5 %collective-permute-start.8 = (f32[160,256]{1,0:T(8,128)S(1)}, f32[160,256]{1,0:T(8,128)S(1)}, u32[]{:S(2)}, u32[]{:S(2)}) collective-permute-start(f32[160,256]{1,0:T(8,128)S(1)} %collective-permute-done.4.refs_3_), channel_id=1, source_target_pairs={{0,16},{16,0},{32,48},{48,32},{64,80},{80,64},{96,112},{112,96},{1... | collective-permute-start | bytes 491528 | tf_op jit(solution)/shard_map/ppermute | solution.py:151
  37.4 3.3 %collective-permute-start.9 = (f32[80,256]{1,0:T(8,128)S(1)}, f32[80,256]{1,0:T(8,128)S(1)}, u32[]{:S(2)}, u32[]{:S(2)}) collective-permute-start(f32[80,256]{1,0:T(8,128)S(1)} %collective-permute-done.5.refs_4_), channel_id=1, source_target_pairs={{0,16},{16,0},{32,48},{48,32},{64,80},{80,64},{96,112},{112,96},{1... | collective-permute-start | bytes 245768 | tf_op jit(solution)/shard_map/ppermute | solution.py:151
  69.7 43.5 %copy-start.8 = (f32[2,256,256]{2,1,0:T(8,128)S(1)}, f32[2,256,256]{2,1,0:T(8,128)}, u32[]{:S(2)}) copy-start(f32[2,256,256]{2,1,0:T(8,128)} %param.7) | copy-start | bytes 1572868
  71.1 2.6 %collective-permute-start.10 = (f32[256,256]{1,0:T(8,128)S(1)}, f32[256,256]{1,0:T(8,128)S(1)}, u32[]{:S(2)}, u32[]{:S(2)}) collective-permute-start(f32[256,256]{1,0:T(8,128)S(1)} %get-tuple-element.21), channel_id=1, source_target_pairs={{0,16},{16,0},{32,48},{48,32},{64,80},{80,64},{96,112},{112,96},{1... | collective-permute-start | bytes 786440 | tf_op jit(solution)/shard_map/ppermute | solution.py:179
  107.6 5.6 %collective-permute-start.11 = (f32[256,256]{1,0:T(8,128)S(1)}, f32[256,256]{1,0:T(8,128)S(1)}, u32[]{:S(2)}, u32[]{:S(2)}) collective-permute-start(f32[256,256]{1,0:T(8,128)S(1)} %bitcast.9), channel_id=1, source_target_pairs={{0,16},{16,0},{32,48},{48,32},{64,80},{80,64},{96,112},{112,96},{1... | collective-permute-start | bytes 786440 | tf_op jit(solution)/shard_map/ppermute | solution.py:185

commit v3 on v2

v3 whole, which is shorter than its diff:
```python
import functools

import jax
import jax.numpy as jnp
from jax import lax
from jax.experimental import pallas as pl
from jax.experimental.pallas import tpu as pltpu
from jax.sharding import PartitionSpec as P

ROW, COL = "prow", "pcol"


def placement(n_row, n_col):
    side = 1
    while side * side < n_col:
        side *= 2
    n_z = n_row // 2
    ring = lambda n, d: min(d % n, -d % n)
    offsets = sorted(range(n_col), key=lambda o: -(ring(side, o // side) + ring(n_col // side, o % side)))
    planes = sorted(range(n_z), key=lambda q: ring(n_z, q))
    table = [0] * n_row
    for n, offset in enumerate(offsets):
        table[2 * planes[n // 2] + n % 2] = offset
    return side, table


def source_of(column, offset, side, n_col):
    wide = n_col // side
    return (column // wide + offset // wide) % side * wide + (column + offset) % wide


def split(x):
    high = x.astype(jnp.bfloat16)
    low = (x - high.astype(jnp.float32)).astype(jnp.bfloat16)
    return high, low


def dot(a, b, contract):
    return lax.dot_general(a, b, ((contract, (0,)), ((), ())), preferred_element_type=jnp.float32)


def dot3(a, b, contract):
    (a_high, a_low), (b_high, b_low) = a, b
    return dot(a_high, b_high, contract) + dot(a_low, b_high, contract) + dot(a_high, b_low, contract)


def in_second(owner_ref, ancestors_ref, stored):
    number = owner_ref[stored]
    found = jnp.int32(0)
    for a in range(ancestors_ref.shape[1]):
        found = found | (ancestors_ref[1, a] == number).astype(jnp.int32)
    return found


def second_rows(block, start, shape, in_first, in_last):
    bound = (start // block + 1) * block - start
    return jnp.where(lax.broadcasted_iota(jnp.int32, shape, 0) < bound, in_first, in_last) == 1


def fetch(pairs, sems):
    copies = [pltpu.make_async_copy(*pair, sems.at[n]) for n, pair in enumerate(pairs)]
    for copy in copies:
        copy.start()
    return copies


def pick_kernel(block, n_col, owner_hbm, ancestors_hbm, panel_hbm, z_ref, owner_ref, ancestors_ref, panel_ref, sems):
    for copy in fetch([(owner_hbm, owner_ref), (ancestors_hbm, ancestors_ref), (panel_hbm, panel_ref)], sems):
        copy.wait()
    rows = z_ref.shape[0]
    start = (lax.axis_index(ROW) * n_col + lax.axis_index(COL)) * rows
    in_first = in_second(owner_ref, ancestors_ref, start // block)
    in_last = in_second(owner_ref, ancestors_ref, (start + rows - 1) // block)
    second = second_rows(block, start, z_ref.shape, in_first, in_last)
    z_ref[...] = jnp.where(second, panel_ref[:, block:], panel_ref[:, :block])


def split_kernel(block, n_col, rows_dev, place, owner_hbm, ancestors_hbm, a_hbm, high_ref, low_ref, sets_ref, owner_ref, ancestors_ref, a_ref, sems):
    n = a_hbm.shape[0] // block
    strips = [pl.ds(b * block, block) for b in range(n)]
    pairs = [(owner_hbm, owner_ref), (ancestors_hbm, ancestors_ref)] + [(a_hbm.at[rows], a_ref.at[rows]) for rows in strips]
    copies = fetch(pairs, sems)
    copies[0].wait()
    copies[1].wait()
    row, col = lax.axis_index(ROW), lax.axis_index(COL)
    start = (row * n_col + col) * rows_dev
    stored = [row * n + b for b in range(n)] + [col * n + b for b in range(n)]
    stored += [start // block, (start + rows_dev - 1) // block]
    for at, which in enumerate(stored):
        sets_ref[at] = in_second(owner_ref, ancestors_ref, which)
    side, table = place
    n_row = len(table)
    for relative, offset in enumerate(table):
        sets_ref[2 * n + 2 + (col // 2 * 2 + relative) % n_row] = source_of(col, offset, side, n_col)
    for copy, rows in zip(copies[2:], strips):
        copy.wait()
        high_ref[rows, :], low_ref[rows, :] = split(a_ref[rows, :])


def product_kernel(block, piece, n_z, sets_ref, high_ref, low_ref, *refs):
    *sources, out_ref, w_ref = refs
    n_blocks = high_ref.shape[0] // block
    row = lax.axis_index(ROW)
    core = row % 2
    steps = [0, 1, 2, 3, 4, 1, 2, 3, 4]
    for n, (source, step) in enumerate(zip(sources, steps)):
        owner = core if n < 5 else 1 - core
        z = (row // 2 + n_z + step * (2 * owner - 1)) % n_z
        for h in range(source.shape[0] // piece):
            start = sets_ref[2 * n_blocks + 2 + 2 * z + (owner ^ h)] * piece
            rows = pl.ds(pl.multiple_of(start, 16), piece)
            in_first = sets_ref[n_blocks + start // block]
            in_last = sets_ref[n_blocks + (start + piece - 1) // block]
            second = second_rows(block, start, (piece, block), in_first, in_last)
            values = source[h * piece : (h + 1) * piece, :]
            for k, kept in enumerate((jnp.where(second, 0.0, values), jnp.where(second, values, 0.0))):
                w_ref[k, 0, rows, :], w_ref[k, 1, rows, :] = split(kept)
    for b in range(n_blocks):
        k = sets_ref[b]
        rows = pl.ds(b * block, block)
        out_ref[rows, :] = -dot3((high_ref[rows, :], low_ref[rows, :]), (w_ref[k, 0], w_ref[k, 1]), (1,))


def finish_kernel(block, n_col, n_blocks, sets_ref, parts_ref, z_ref, column_ref, keep_ref, send_ref):
    y = parts_ref[0]
    for s in range(1, parts_ref.shape[0]):
        y = y + parts_ref[s]
    start = (lax.axis_index(ROW) * n_col + lax.axis_index(COL)) * y.shape[0]
    second = second_rows(block, start, y.shape, sets_ref[2 * n_blocks], sets_ref[2 * n_blocks + 1])
    column_ref[:, :block] = jnp.where(second, 0.0, y)
    column_ref[:, block:] = jnp.where(second, y, 0.0)
    z = z_ref[...]
    kept = second == (lax.axis_index(ROW) % 2 == 1)
    y = split(y)
    keep_ref[...] = dot3(split(jnp.where(kept, z, 0.0)), y, (0,))
    send_ref[...] = dot3(split(jnp.where(kept, 0.0, z)), y, (0,))


def per_device(inverse_block, l_panel, d_inverse, owner_map, ancestors):
    block = d_inverse.shape[1]
    rows_dev = l_panel.shape[0]
    n_row = lax.axis_size(ROW)
    n_col = lax.axis_size(COL)
    edge = inverse_block.shape[0]
    n_blocks = edge // block
    n_z = n_row // 2
    f32 = jnp.float32
    smem = pl.BlockSpec(memory_space=pltpu.SMEM)
    vmem = pl.BlockSpec(memory_space=pltpu.VMEM)
    limit = lambda mib: mib * 1024 * 1024
    swap = [(i, i ^ 1) for i in range(n_row)]
    groups = [list(range(c, n_row, 2)) for c in range(2)]

    hbm = pl.BlockSpec(memory_space=pltpu.HBM)
    small = [
        pltpu.SMEM(owner_map.shape, jnp.int32),
        pltpu.SMEM(ancestors.shape, jnp.int32),
    ]
    z = pl.pallas_call(
        functools.partial(pick_kernel, block, n_col),
        out_shape=jax.ShapeDtypeStruct((rows_dev, block), f32),
        in_specs=[hbm, hbm, hbm],
        out_specs=vmem,
        scratch_shapes=[*small, pltpu.VMEM(l_panel.shape, f32), pltpu.SemaphoreType.DMA((3,))],
        compiler_params=pltpu.CompilerParams(vmem_limit_bytes=limit(60)),
    )(owner_map, ancestors, l_panel)
    side, table = place = placement(n_row, n_col)
    targets = {}
    for j in range(n_row):
        for relative, offset in enumerate(table):
            targets[j, source_of(j, offset, side, n_col)] = (j // 2 * 2 + relative) % n_row
    turned = lax.ppermute(z, (ROW, COL), [(j * n_col + s, p * n_col + j) for (j, s), p in targets.items()])
    high, low, sets = pl.pallas_call(
        functools.partial(split_kernel, block, n_col, rows_dev, place),
        out_shape=[
            jax.ShapeDtypeStruct((edge, edge), jnp.bfloat16),
            jax.ShapeDtypeStruct((edge, edge), jnp.bfloat16),
            jax.ShapeDtypeStruct((2 * n_blocks + 2 + n_row,), jnp.int32),
        ],
        in_specs=[hbm, hbm, hbm],
        out_specs=[vmem, vmem, smem],
        scratch_shapes=[*small, pltpu.VMEM((edge, edge), f32), pltpu.SemaphoreType.DMA((n_blocks + 2,))],
        compiler_params=pltpu.CompilerParams(vmem_limit_bytes=limit(44)),
        cost_estimate=pl.CostEstimate(flops=4 * edge * edge, bytes_accessed=8 * edge * edge, transcendentals=0),
    )(owner_map, ancestors, inverse_block)
    turned, high, low, sets = lax.optimization_barrier((turned, high, low, sets))

    def along(x, step):
        pairs = [(2 * q + c, 2 * ((q + step * (1 - 2 * c)) % n_z) + c) for q in range(n_z) for c in range(2)]
        return lax.ppermute(x, ROW, pairs)

    chunk = jnp.concatenate([turned, lax.ppermute(turned, ROW, swap)])
    one, two = along(chunk, 1), along(chunk, 2)
    three, four = along(two, 1), along(two[:rows_dev], 2)
    pieces = [one, two, three, four]
    pieces = [chunk, *pieces, *(lax.ppermute(p, ROW, swap) for p in pieces)]

    sent = pl.pallas_call(
        functools.partial(product_kernel, block, rows_dev, n_z),
        out_shape=jax.ShapeDtypeStruct((edge, block), f32),
        in_specs=[smem, vmem, vmem] + [vmem] * len(pieces),
        out_specs=vmem,
        scratch_shapes=[pltpu.VMEM((2, 2, edge, block), jnp.bfloat16)],
        compiler_params=pltpu.CompilerParams(vmem_limit_bytes=limit(20)),
        cost_estimate=pl.CostEstimate(
            flops=6 * edge * edge * block, bytes_accessed=4 * edge * (edge + 2 * block), transcendentals=0
        ),
    )(sets, high, low, *pieces)
    parts = lax.all_to_all(sent.reshape(n_col, rows_dev, block), COL, 0, 0)

    column, keep, send = pl.pallas_call(
        functools.partial(finish_kernel, block, n_col, n_blocks),
        out_shape=[
            jax.ShapeDtypeStruct((rows_dev, 2 * block), f32),
            jax.ShapeDtypeStruct((block, block), f32),
            jax.ShapeDtypeStruct((block, block), f32),
        ],
        in_specs=[smem, vmem, vmem],
        out_specs=[vmem, vmem, vmem],
        compiler_params=pltpu.CompilerParams(vmem_limit_bytes=limit(12)),
    )(sets, parts, z)

    per = block // n_col
    terms = keep + lax.ppermute(send, ROW, swap)
    terms = jnp.sum(lax.all_to_all(terms.reshape(n_col, per, block), COL, 0, 0), axis=0)
    terms = jnp.broadcast_to(terms[None], (n_z, per, block))
    terms = jnp.sum(lax.all_to_all(terms, ROW, 0, 0, axis_index_groups=groups), axis=0)
    terms = jnp.broadcast_to(terms[None], (n_col, per, block))
    here = lax.all_to_all(terms, COL, 0, 0).reshape(block, block)
    there = lax.ppermute(here, ROW, swap)
    first = lax.axis_index(ROW) % 2 == 0
    diag = d_inverse - jnp.stack([jnp.where(first, here, there), jnp.where(first, there, here)])
    return column, diag


def solution(mesh):
    return jax.shard_map(
        per_device,
        mesh=mesh,
        in_specs=(P(ROW, COL), P((ROW, COL), None), P(), P(), P()),
        out_specs=(P((ROW, COL), None), P()),
        check_vma=False,
    )
```

time: 114 us -> 110 us (0.965)
  local copies, waits for them, and re-layouts: 6.49 us -> 1.39 us
  Pallas kernels: 8.2 us -> 10.2 us
    ppermute x4, starting transfers between devices: 16.1 us -> 10.4 us  [along(): return lax.ppermute(x, ROW, pairs)]
    unnamed x19 -> x9, local copies, waits for them, and re-layouts: 6.45 us -> 1.35 us
    ppermute x1, starting transfers between devices: 3.95 us -> 8.87 us  [per_device(): lax.ppermute(z, (ROW, COL), [(j * n_col + s, p * n_col + j) for (j, s), p...]
  transfers between devices with their start and end apart: 12 -> 12, of which waited for: 5 -> 6; matrix products, arithmetic and copies ran while one was open for 0% -> 0% of each run, Pallas kernels for 2% -> 3%
where the time goes in v3:
time: 110 us
  blocking collectives  58.5 us (53%)
  starting transfers between devices  31.3 us (28%)
  Pallas kernels  10.2 us (9%)
  waiting for transfers between devices  6.6 us (6%)
  local copies, waits for them, and re-layouts  1.39 us (1%)
    all_to_all x1, blocking collectives, per_device(): parts = lax.all_to_all(sent.reshape(n_col, rows_dev, block), COL, 0, 0)  24.4 us
    all_to_all x1, blocking collectives, per_device(): lax.all_to_all(terms, ROW, 0, 0, axis_index_groups=groups)  13.2 us
    all_to_all x1, blocking collectives, per_device(): lax.all_to_all(terms.reshape(n_col, per, block), COL, 0, 0)  10.7 us
    ppermute x4, starting transfers between devices, along(): return lax.ppermute(x, ROW, pairs)  10.4 us
    all_to_all x1, blocking collectives, per_device(): here = lax.all_to_all(terms, COL, 0, 0).reshape(block, block)  10.1 us
    ppermute x1, starting transfers between devices, per_device(): lax.ppermute(z, (ROW, COL), [(j * n_col + s, p * n_col + j) for (j, s), p...  8.87 us
    ppermute x4, starting transfers between devices, per_device(): pieces = [chunk, *pieces, *(lax.ppermute(p, ROW, swap) for p in pieces)]  6.02 us
    ppermute x1, starting transfers between devices, per_device(): there = lax.ppermute(here, ROW, swap)  4.4 us
  transfers between devices with their start and end apart: 12, of which 6 were waited for; matrix products, arithmetic and copies ran while one was open for 0% of the time, Pallas kernels for 3%

profile of v3, /device:TPU:1, one launch (start us, length us, event | category | flops | bytes accessed | tf_op | source)
XLA Modules:
  0.0 109.7 jit_solution(11757278636315110560)
XLA Ops:
  0.6 1.6 %shard_map.68.z_ref = f32[80,256]{1,0:T(8,128)} custom-call(s32[80]{0:T(128)} %owner_hbm.3, s32[2,40]{1,0:T(2,128)} %ancestors_hbm.3, f32[80,512]{1,0:T(8,128)} %panel_hbm.1), custom_call_target="tpu_custom_call" | custom-call | tf_op jit(solution)/shard_map/pallas_call | solution.py:159
  2.2 8.9 %collective-permute-start = (f32[80,256]{1,0:T(8,128)}, f32[80,256]{1,0:T(8,128)S(1)}, u32[]{:S(2)}, u32[]{:S(2)}) collective-permute-start(f32[80,256]{1,0:T(8,128)} %shard_map.68.z_ref), channel_id=1, source_target_pairs={{10,0},{6,16},{9,32},{11,48},{5,64},{7,80},{15,96},{1,112},{12,128... | collective-permute-start | bytes 245768 | tf_op jit(solution)/shard_map/ppermute | solution.py:172
  11.1 0.0 copy-start.1
  11.1 0.7 copy-done.1
  11.8 0.0 copy-start.2
  11.8 0.7 copy-done.2
  12.4 3.5 %shard_map.69 = (bf16[1280,1280]{1,0:T(8,128)(2,1)S(1)}, bf16[1280,1280]{1,0:T(8,128)(2,1)S(1)}, s32[28]{0:T(128)S(1)}) custom-call(s32[80]{0:T(128)S(1)} %copy-done.2, s32[2,40]{1,0:T(2,128)S(1)} %copy-done.1, f32[1280,1280]{1,0:T(8,128)} %a_hbm.1), custom_call_target="tpu_custom_call" | custom-call | flops 6553600 | bytes 13107200 | tf_op jit(solution)/shard_map/pallas_call | solution.py:173
  16.0 0.0 collective-permute-done
  16.0 0.1 collective-permute-start.1
  16.1 1.2 %collective-permute-done.1 = f32[80,256]{1,0:T(8,128)S(1)} collective-permute-done((f32[80,256]{1,0:T(8,128)S(1)}, f32[80,256]{1,0:T(8,128)S(1)}, u32[]{:S(2)}, u32[]{:S(2)}) %collective-permute-start.1) | collective-permute-done | bytes 81952 | tf_op jit(solution)/shard_map/ppermute | solution.py:192
  17.4 3.3 %collective-permute-start.3 = (f32[160,256]{1,0:T(8,128)S(1)}, f32[160,256]{1,0:T(8,128)S(1)}, u32[]{:S(2)}, u32[]{:S(2)}) collective-permute-start(f32[160,256]{1,0:T(8,128)S(1)} %constant_dynamic-update-slice_fusion.refs_0_), channel_id=1, source_target_pairs={{0,64},{16,208},{32,96},{48,240},{64,128},{80,16},{96,160},{112,48... | collective-permute-start | bytes 491528 | tf_op jit(solution)/shard_map/ppermute | solution.py:190
  20.7 1.9 %collective-permute-start.2 = (f32[160,256]{1,0:T(8,128)S(1)}, f32[160,256]{1,0:T(8,128)S(1)}, u32[]{:S(2)}, u32[]{:S(2)}) collective-permute-start(f32[160,256]{1,0:T(8,128)S(1)} %constant_dynamic-update-slice_fusion.refs_0_), channel_id=1, source_target_pairs={{0,32},{16,240},{32,64},{48,16},{64,96},{80,48},{96,128},{112,80},... | collective-permute-start | bytes 491528 | tf_op jit(solution)/shard_map/ppermute | solution.py:190
  22.6 1.9 %collective-permute-done.3.refs_2_ = f32[160,256]{1,0:T(8,128)S(1)} collective-permute-done((f32[160,256]{1,0:T(8,128)S(1)}, f32[160,256]{1,0:T(8,128)S(1)}, u32[]{:S(2)}, u32[]{:S(2)}) %collective-permute-start.3) | collective-permute-done | bytes 163872 | tf_op jit(solution)/shard_map/ppermute | solution.py:190
  24.6 3.2 %collective-permute-start.4 = (f32[160,256]{1,0:T(8,128)S(1)}, f32[160,256]{1,0:T(8,128)S(1)}, u32[]{:S(2)}, u32[]{:S(2)}) collective-permute-start(f32[160,256]{1,0:T(8,128)S(1)} %collective-permute-done.3.refs_2_), channel_id=1, source_target_pairs={{0,32},{16,240},{32,64},{48,16},{64,96},{80,48},{96,128},{112,80},... | collective-permute-start | bytes 491528 | tf_op jit(solution)/shard_map/ppermute | solution.py:190
  27.7 0.0 copy-start
  27.7 2.0 %collective-permute-start.5 = (f32[80,256]{1,0:T(8,128)S(1)}, f32[80,256]{1,0:T(8,128)S(1)}, u32[]{:S(2)}, u32[]{:S(2)}) collective-permute-start(f32[80,256]{1,0:T(8,128)S(1)} %slice.4), channel_id=1, source_target_pairs={{0,64},{16,208},{32,96},{48,240},{64,128},{80,16},{96,160},{112,48... | collective-permute-start | bytes 245768 | tf_op jit(solution)/shard_map/ppermute | solution.py:190
  29.7 0.0 collective-permute-start.7
  29.7 0.0 collective-permute-done.2.refs_1_
  29.7 0.5 collective-permute-start.6
  30.2 0.0 collective-permute-done.4.refs_3_
  30.2 2.5 %collective-permute-start.8 = (f32[160,256]{1,0:T(8,128)S(1)}, f32[160,256]{1,0:T(8,128)S(1)}, u32[]{:S(2)}, u32[]{:S(2)}) collective-permute-start(f32[160,256]{1,0:T(8,128)S(1)} %collective-permute-done.4.refs_3_), channel_id=1, source_target_pairs={{0,16},{16,0},{32,48},{48,32},{64,80},{80,64},{96,112},{112,96},{1... | collective-permute-start | bytes 491528 | tf_op jit(solution)/shard_map/ppermute | solution.py:196
  32.7 0.2 collective-permute-done.5.refs_4_
  32.9 3.0 %collective-permute-start.9 = (f32[80,256]{1,0:T(8,128)S(1)}, f32[80,256]{1,0:T(8,128)S(1)}, u32[]{:S(2)}, u32[]{:S(2)}) collective-permute-start(f32[80,256]{1,0:T(8,128)S(1)} %collective-permute-done.5.refs_4_), channel_id=1, source_target_pairs={{0,16},{16,0},{32,48},{48,32},{64,80},{80,64},{96,112},{112,96},{1... | collective-permute-start | bytes 245768 | tf_op jit(solution)/shard_map/ppermute | solution.py:196
  35.9 0.9 collective-permute-done.9.refs_8_
  36.8 0.0 collective-permute-done.7.refs_6_
  36.9 0.0 collective-permute-done.6.refs_5_
  36.9 0.0 collective-permute-done.8.refs_7_
  36.9 3.8 %shard_map.70 = f32[1280,256]{1,0:T(8,128)S(1)} custom-call(s32[28]{0:T(128)S(1)} %get-tuple-element.15.sets_ref, bf16[1280,1280]{1,0:T(8,128)(2,1)S(1)} %get-tuple-element.16.high_ref, bf16[1280,1280]{1,0:T(8,128)(2,1)S(1)} %get-tuple-element.17.low_ref, f32[160,256]{1,0:T(8,128)S(1)} %constant_dynamic-update-slice_fusion.refs_0_, ...), custom_call_target="tpu_custom_call" | custom-call | flops 2516582400 | bytes 9175040 | tf_op jit(solution)/shard_map/pallas_call | solution.py:198
  40.6 24.4 %all_to_all.20.parts_ref = f32[16,80,256]{2,1,0:T(8,128)S(1)} all-to-all(f32[16,80,256]{2,1,0:T(8,128)S(1)} %bitcast.9), channel_id=1, replica_groups=mesh['prow'=16,'pcol'=16] {'pcol'}, dimensions={0} | all-to-all | bytes 2621440 | tf_op jit(solution)/shard_map/all_to_all | solution.py:209
  65.0 0.0 copy-done
  65.0 0.0 copy-start.3
  65.0 1.3 %shard_map.71 = (f32[80,512]{1,0:T(8,128)}, f32[256,256]{1,0:T(8,128)S(1)}, f32[256,256]{1,0:T(8,128)S(1)}) custom-call(s32[28]{0:T(128)S(1)} %get-tuple-element.15.sets_ref, f32[16,80,256]{2,1,0:T(8,128)S(1)} %all_to_all.20.parts_ref, f32[80,256]{1,0:T(8,128)S(1)} %copy-done), custom_call_target="tpu_custom_call" | custom-call | tf_op jit(solution)/shard_map/pallas_call | solution.py:211
  66.3 1.5 %collective-permute-start.10 = (f32[256,256]{1,0:T(8,128)S(1)}, f32[256,256]{1,0:T(8,128)S(1)}, u32[]{:S(2)}, u32[]{:S(2)}) collective-permute-start(f32[256,256]{1,0:T(8,128)S(1)} %get-tuple-element.21), channel_id=1, source_target_pairs={{0,16},{16,0},{32,48},{48,32},{64,80},{80,64},{96,112},{112,96},{1... | collective-permute-start | bytes 786440 | tf_op jit(solution)/shard_map/ppermute | solution.py:224
  67.8 1.2 %collective-permute-done.10 = f32[256,256]{1,0:T(8,128)S(1)} collective-permute-done((f32[256,256]{1,0:T(8,128)S(1)}, f32[256,256]{1,0:T(8,128)S(1)}, u32[]{:S(2)}, u32[]{:S(2)}) %collective-permute-start.10) | collective-permute-done | bytes 262176 | tf_op jit(solution)/shard_map/ppermute | solution.py:224
  69.0 10.7 %all_to_all.21 = f32[16,16,256]{2,1,0:T(8,128)S(1)} all-to-all(f32[16,16,256]{2,1,0:T(8,128)S(1)} %bitcast.10), channel_id=1, replica_groups=mesh['prow'=16,'pcol'=16] {'pcol'}, dimensions={0} | all-to-all | bytes 524288 | tf_op jit(solution)/shard_map/all_to_all | solution.py:225
  79.8 13.2 %all_to_all.22 = f32[8,16,256]{2,1,0:T(8,128)S(1)} all-to-all(f32[8,16,256]{2,1,0:T(8,128)S(1)} %broadcast_in_dim.4), channel_id=1, replica_groups={{0,32,64,96,128,160,192,224},{16,48,80,112,144,176,208,240},{1,33,65,97..., dimensions={0} | all-to-all | bytes 262144 | tf_op jit(solution)/shard_map/all_to_all | solution.py:227
  93.0 10.1 %all_to_all.23 = f32[16,16,256]{2,1,0:T(8,128)S(1)} all-to-all(f32[16,16,256]{2,1,0:T(8,128)S(1)} %broadcast_in_dim.5), channel_id=1, replica_groups=mesh['prow'=16,'pcol'=16] {'pcol'}, dimensions={0} | all-to-all | bytes 524288 | tf_op jit(solution)/shard_map/all_to_all | solution.py:229
  103.2 4.4 %collective-permute-start.11 = (f32[256,256]{1,0:T(8,128)S(1)}, f32[256,256]{1,0:T(8,128)S(1)}, u32[]{:S(2)}, u32[]{:S(2)}) collective-permute-start(f32[256,256]{1,0:T(8,128)S(1)} %bitcast.11), channel_id=1, source_target_pairs={{0,16},{16,0},{32,48},{48,32},{64,80},{80,64},{96,112},{112,96},{1... | collective-permute-start | bytes 786440 | tf_op jit(solution)/shard_map/ppermute | solution.py:230
  107.6 1.2 %collective-permute-done.11 = f32[256,256]{1,0:T(8,128)S(1)} collective-permute-done((f32[256,256]{1,0:T(8,128)S(1)}, f32[256,256]{1,0:T(8,128)S(1)}, u32[]{:S(2)}, u32[]{:S(2)}) %collective-permute-start.11) | collective-permute-done | bytes 262176 | tf_op jit(solution)/shard_map/ppermute | solution.py:230
  108.8 0.0 copy-done.3
  108.8 0.9 maximum_subtract_fusion
  (9 shorter events, 0.2 us)
Async XLA Ops:
  2.2 13.8 %collective-permute-start = (f32[80,256]{1,0:T(8,128)}, f32[80,256]{1,0:T(8,128)S(1)}, u32[]{:S(2)}, u32[]{:S(2)}) collective-permute-start(f32[80,256]{1,0:T(8,128)} %shard_map.68.z_ref), channel_id=1, source_target_pairs={{10,0},{6,16},{9,32},{11,48},{5,64},{7,80},{15,96},{1,112},{12,128... | collective-permute-start | bytes 245768 | tf_op jit(solution)/shard_map/ppermute | solution.py:172
  11.1 0.7 copy-start.1
  11.8 0.7 copy-start.2
  16.0 1.4 %collective-permute-start.1 = (f32[80,256]{1,0:T(8,128)S(1)}, f32[80,256]{1,0:T(8,128)S(1)}, u32[]{:S(2)}, u32[]{:S(2)}) collective-permute-start(f32[80,256]{1,0:T(8,128)S(1)} %collective-permute-done), channel_id=1, source_target_pairs={{0,16},{16,0},{32,48},{48,32},{64,80},{80,64},{96,112},{112,96},{1... | collective-permute-start | bytes 245768 | tf_op jit(solution)/shard_map/ppermute | solution.py:192
  17.4 7.2 %collective-permute-start.3 = (f32[160,256]{1,0:T(8,128)S(1)}, f32[160,256]{1,0:T(8,128)S(1)}, u32[]{:S(2)}, u32[]{:S(2)}) collective-permute-start(f32[160,256]{1,0:T(8,128)S(1)} %constant_dynamic-update-slice_fusion.refs_0_), channel_id=1, source_target_pairs={{0,64},{16,208},{32,96},{48,240},{64,128},{80,16},{96,160},{112,48... | collective-permute-start | bytes 491528 | tf_op jit(solution)/shard_map/ppermute | solution.py:190
  20.7 9.0 %collective-permute-start.2 = (f32[160,256]{1,0:T(8,128)S(1)}, f32[160,256]{1,0:T(8,128)S(1)}, u32[]{:S(2)}, u32[]{:S(2)}) collective-permute-start(f32[160,256]{1,0:T(8,128)S(1)} %constant_dynamic-update-slice_fusion.refs_0_), channel_id=1, source_target_pairs={{0,32},{16,240},{32,64},{48,16},{64,96},{80,48},{96,128},{112,80},... | collective-permute-start | bytes 491528 | tf_op jit(solution)/shard_map/ppermute | solution.py:190
  24.6 5.7 %collective-permute-start.4 = (f32[160,256]{1,0:T(8,128)S(1)}, f32[160,256]{1,0:T(8,128)S(1)}, u32[]{:S(2)}, u32[]{:S(2)}) collective-permute-start(f32[160,256]{1,0:T(8,128)S(1)} %collective-permute-done.3.refs_2_), channel_id=1, source_target_pairs={{0,32},{16,240},{32,64},{48,16},{64,96},{80,48},{96,128},{112,80},... | collective-permute-start | bytes 491528 | tf_op jit(solution)/shard_map/ppermute | solution.py:190
  27.7 37.3 %copy-start = (f32[80,256]{1,0:T(8,128)S(1)}, f32[80,256]{1,0:T(8,128)}, u32[]{:S(2)}) copy-start(f32[80,256]{1,0:T(8,128)} %shard_map.68.z_ref) | copy-start | bytes 245764
  27.7 5.1 %collective-permute-start.5 = (f32[80,256]{1,0:T(8,128)S(1)}, f32[80,256]{1,0:T(8,128)S(1)}, u32[]{:S(2)}, u32[]{:S(2)}) collective-permute-start(f32[80,256]{1,0:T(8,128)S(1)} %slice.4), channel_id=1, source_target_pairs={{0,64},{16,208},{32,96},{48,240},{64,128},{80,16},{96,160},{112,48... | collective-permute-start | bytes 245768 | tf_op jit(solution)/shard_map/ppermute | solution.py:190
  29.7 7.1 %collective-permute-start.7 = (f32[160,256]{1,0:T(8,128)S(1)}, f32[160,256]{1,0:T(8,128)S(1)}, u32[]{:S(2)}, u32[]{:S(2)}) collective-permute-start(f32[160,256]{1,0:T(8,128)S(1)} %collective-permute-done.3.refs_2_), channel_id=1, source_target_pairs={{0,16},{16,0},{32,48},{48,32},{64,80},{80,64},{96,112},{112,96},{1... | collective-permute-start | bytes 491528 | tf_op jit(solution)/shard_map/ppermute | solution.py:196
  29.7 7.1 %collective-permute-start.6 = (f32[160,256]{1,0:T(8,128)S(1)}, f32[160,256]{1,0:T(8,128)S(1)}, u32[]{:S(2)}, u32[]{:S(2)}) collective-permute-start(f32[160,256]{1,0:T(8,128)S(1)} %collective-permute-done.2.refs_1_), channel_id=1, source_target_pairs={{0,16},{16,0},{32,48},{48,32},{64,80},{80,64},{96,112},{112,96},{1... | collective-permute-start | bytes 491528 | tf_op jit(solution)/shard_map/ppermute | solution.py:196
  30.2 6.6 %collective-permute-start.8 = (f32[160,256]{1,0:T(8,128)S(1)}, f32[160,256]{1,0:T(8,128)S(1)}, u32[]{:S(2)}, u32[]{:S(2)}) collective-permute-start(f32[160,256]{1,0:T(8,128)S(1)} %collective-permute-done.4.refs_3_), channel_id=1, source_target_pairs={{0,16},{16,0},{32,48},{48,32},{64,80},{80,64},{96,112},{112,96},{1... | collective-permute-start | bytes 491528 | tf_op jit(solution)/shard_map/ppermute | solution.py:196
  32.9 4.0 %collective-permute-start.9 = (f32[80,256]{1,0:T(8,128)S(1)}, f32[80,256]{1,0:T(8,128)S(1)}, u32[]{:S(2)}, u32[]{:S(2)}) collective-permute-start(f32[80,256]{1,0:T(8,128)S(1)} %collective-permute-done.5.refs_4_), channel_id=1, source_target_pairs={{0,16},{16,0},{32,48},{48,32},{64,80},{80,64},{96,112},{112,96},{1... | collective-permute-start | bytes 245768 | tf_op jit(solution)/shard_map/ppermute | solution.py:196
  65.0 43.7 %copy-start.3 = (f32[2,256,256]{2,1,0:T(8,128)S(1)}, f32[2,256,256]{2,1,0:T(8,128)}, u32[]{:S(2)}) copy-start(f32[2,256,256]{2,1,0:T(8,128)} %param.7) | copy-start | bytes 1572868
  66.3 2.6 %collective-permute-start.10 = (f32[256,256]{1,0:T(8,128)S(1)}, f32[256,256]{1,0:T(8,128)S(1)}, u32[]{:S(2)}, u32[]{:S(2)}) collective-permute-start(f32[256,256]{1,0:T(8,128)S(1)} %get-tuple-element.21), channel_id=1, source_target_pairs={{0,16},{16,0},{32,48},{48,32},{64,80},{80,64},{96,112},{112,96},{1... | collective-permute-start | bytes 786440 | tf_op jit(solution)/shard_map/ppermute | solution.py:224
  103.2 5.6 %collective-permute-start.11 = (f32[256,256]{1,0:T(8,128)S(1)}, f32[256,256]{1,0:T(8,128)S(1)}, u32[]{:S(2)}, u32[]{:S(2)}) collective-permute-start(f32[256,256]{1,0:T(8,128)S(1)} %bitcast.11), channel_id=1, source_target_pairs={{0,16},{16,0},{32,48},{48,32},{64,80},{80,64},{96,112},{112,96},{1... | collective-permute-start | bytes 786440 | tf_op jit(solution)/shard_map/ppermute | solution.py:230

commit v4 on v3

--- a/solution.py
+++ b/solution.py
@@ -121,19 +121,37 @@
         out_ref[rows, :] = -dot3((high_ref[rows, :], low_ref[rows, :]), (w_ref[k, 0], w_ref[k, 1]), (1,))
 
 
-def finish_kernel(block, n_col, n_blocks, sets_ref, parts_ref, z_ref, column_ref, keep_ref, send_ref):
+def rows_terms(block, n_col, n_blocks, sets_ref, z_ref, y, of_sibling):
+    start = (lax.axis_index(ROW) * n_col + lax.axis_index(COL)) * y.shape[0]
+    second = second_rows(block, start, y.shape, sets_ref[2 * n_blocks], sets_ref[2 * n_blocks + 1])
+    kept = second == ((lax.axis_index(ROW) + of_sibling) % 2 == 1)
+    return second, dot3(split(jnp.where(kept, z_ref[...], 0.0)), split(y), (0,))
+
+
+def send_kernel(block, n_col, n_blocks, sets_ref, parts_ref, z_ref, y_ref, send_ref):
     y = parts_ref[0]
     for s in range(1, parts_ref.shape[0]):
         y = y + parts_ref[s]
+    y_ref[...] = y
+    send_ref[...] = rows_terms(block, n_col, n_blocks, sets_ref, z_ref, y, 1)[1]
+
+
+def keep_kernel(block, n_col, n_blocks, sets_ref, y_ref, z_ref, keep_ref):
+    keep_ref[...] = rows_terms(block, n_col, n_blocks, sets_ref, z_ref, y_ref[...], 0)[1]
+
+
+def column_kernel(block, n_col, n_blocks, sets_ref, y_ref, column_ref):
+    y = y_ref[...]
     start = (lax.axis_index(ROW) * n_col + lax.axis_index(COL)) * y.shape[0]
     second = second_rows(block, start, y.shape, sets_ref[2 * n_blocks], sets_ref[2 * n_blocks + 1])
     column_ref[:, :block] = jnp.where(second, 0.0, y)
     column_ref[:, block:] = jnp.where(second, y, 0.0)
-    z = z_ref[...]
-    kept = second == (lax.axis_index(ROW) % 2 == 1)
-    y = split(y)
-    keep_ref[...] = dot3(split(jnp.where(kept, z, 0.0)), y, (0,))
-    send_ref[...] = dot3(split(jnp.where(kept, 0.0, z)), y, (0,))
+
+
+def last_kernel(d_ref, here_ref, there_ref, out_ref):
+    core = lax.axis_index(ROW) % 2
+    out_ref[core] = d_ref[core] - here_ref[...]
+    out_ref[1 - core] = d_ref[1 - core] - there_ref[...]
 
 
 def per_device(inverse_block, l_panel, d_inverse, owner_map, ancestors):
@@ -208,17 +226,22 @@
     )(sets, high, low, *pieces)
     parts = lax.all_to_all(sent.reshape(n_col, rows_dev, block), COL, 0, 0)
 
-    column, keep, send = pl.pallas_call(
-        functools.partial(finish_kernel, block, n_col, n_blocks),
-        out_shape=[
-            jax.ShapeDtypeStruct((rows_dev, 2 * block), f32),
-            jax.ShapeDtypeStruct((block, block), f32),
-            jax.ShapeDtypeStruct((block, block), f32),
-        ],
+    square = jax.ShapeDtypeStruct((block, block), f32)
+    small_limit = pltpu.CompilerParams(vmem_limit_bytes=limit(12))
+    y, send = pl.pallas_call(
+        functools.partial(send_kernel, block, n_col, n_blocks),
+        out_shape=[jax.ShapeDtypeStruct((rows_dev, block), f32), square],
         in_specs=[smem, vmem, vmem],
-        out_specs=[vmem, vmem, vmem],
-        compiler_params=pltpu.CompilerParams(vmem_limit_bytes=limit(12)),
+        out_specs=[vmem, vmem],
+        compiler_params=small_limit,
     )(sets, parts, z)
+    keep = pl.pallas_call(
+        functools.partial(keep_kernel, block, n_col, n_blocks),
+        out_shape=square,
+        in_specs=[smem, vmem, vmem],
+        out_specs=vmem,
+        compiler_params=small_limit,
+    )(sets, y, z)
 
     per = block // n_col
     terms = keep + lax.ppermute(send, ROW, swap)
@@ -228,8 +251,22 @@
     terms = jnp.broadcast_to(terms[None], (n_col, per, block))
     here = lax.all_to_all(terms, COL, 0, 0).reshape(block, block)
     there = lax.ppermute(here, ROW, swap)
-    first = lax.axis_index(ROW) % 2 == 0
-    diag = d_inverse - jnp.stack([jnp.where(first, here, there), jnp.where(first, there, here)])
+    y, here = lax.optimization_barrier((y, here))
+    column = pl.pallas_call(
+        functools.partial(column_kernel, block, n_col, n_blocks),
+        out_shape=jax.ShapeDtypeStruct((rows_dev, 2 * block), f32),
+        in_specs=[smem, vmem],
+        out_specs=vmem,
+        compiler_params=small_limit,
+    )(sets, y)
+    there, column = lax.optimization_barrier((there, column))
+    diag = pl.pallas_call(
+        last_kernel,
+        out_shape=jax.ShapeDtypeStruct(d_inverse.shape, f32),
+        in_specs=[vmem, vmem, vmem],
+        out_specs=vmem,
+        compiler_params=small_limit,
+    )(d_inverse, here, there)
     return column, diag
 
 

time: 110 us -> 110 us (level)
  Pallas kernels: 10.2 us -> 12.7 us
  waiting for transfers between devices: 6.6 us -> 4.59 us
    pallas_call x1 -> x4, Pallas kernels: 1.29 us -> 3.8 us  [the longest x1 1.24 us: per_device(): pl.pallas_call(functools.partial(column_kernel, block, n_col, n_blocks),...]
    ppermute x1, waiting for transfers between devices: 1.16 us -> 0.01 us  [per_device(): there = lax.ppermute(here, ROW, swap)]
  transfers between devices with their start and end apart: 12 -> 12, of which waited for: 6 -> 5; matrix products, arithmetic and copies ran while one was open for 0% -> 0% of each run, Pallas kernels for 3% -> 5%
where the time goes in v4:
time: 110 us; the launch traced here: 109 us
  blocking collectives  58.6 us (53%)
  starting transfers between devices  31.3 us (28%)
  Pallas kernels  12.7 us (12%)
  waiting for transfers between devices  4.59 us (4%)
  local copies, waits for them, and re-layouts  1.39 us (1%)
    all_to_all x1, blocking collectives, per_device(): parts = lax.all_to_all(sent.reshape(n_col, rows_dev, block), COL, 0, 0)  24.5 us
    all_to_all x1, blocking collectives, per_device(): lax.all_to_all(terms, ROW, 0, 0, axis_index_groups=groups)  13.2 us
    all_to_all x1, blocking collectives, per_device(): lax.all_to_all(terms.reshape(n_col, per, block), COL, 0, 0)  10.7 us
    ppermute x4, starting transfers between devices, along(): return lax.ppermute(x, ROW, pairs)  10.4 us
    all_to_all x1, blocking collectives, per_device(): here = lax.all_to_all(terms, COL, 0, 0).reshape(block, block)  10.1 us
    ppermute x1, starting transfers between devices, per_device(): lax.ppermute(z, (ROW, COL), [(j * n_col + s, p * n_col + j) for (j, s), p...  8.87 us
    ppermute x4, starting transfers between devices, per_device(): pieces = [chunk, *pieces, *(lax.ppermute(p, ROW, swap) for p in pieces)]  6.02 us
    ppermute x1, starting transfers between devices, per_device(): there = lax.ppermute(here, ROW, swap)  4.4 us
  transfers between devices with their start and end apart: 12, of which 5 were waited for; matrix products, arithmetic and copies ran while one was open for 0% of the time, Pallas kernels for 5%

profile of v4, /device:TPU:1, one launch (start us, length us, event | category | flops | bytes accessed | tf_op | source)
XLA Modules:
  0.0 109.5 jit_solution(5996126793650353628)
XLA Ops:
  0.6 1.6 %shard_map.68.z_ref = f32[80,256]{1,0:T(8,128)} custom-call(s32[80]{0:T(128)} %owner_hbm.3, s32[2,40]{1,0:T(2,128)} %ancestors_hbm.3, f32[80,512]{1,0:T(8,128)} %panel_hbm.1), custom_call_target="tpu_custom_call" | custom-call | tf_op jit(solution)/shard_map/pallas_call | solution.py:177
  2.2 8.9 %collective-permute-start = (f32[80,256]{1,0:T(8,128)}, f32[80,256]{1,0:T(8,128)S(1)}, u32[]{:S(2)}, u32[]{:S(2)}) collective-permute-start(f32[80,256]{1,0:T(8,128)} %shard_map.68.z_ref), channel_id=1, source_target_pairs={{10,0},{6,16},{9,32},{11,48},{5,64},{7,80},{15,96},{1,112},{12,128... | collective-permute-start | bytes 245768 | tf_op jit(solution)/shard_map/ppermute | solution.py:190
  11.1 0.0 copy-start.2
  11.1 0.7 copy-done.2
  11.8 0.0 copy-start.3
  11.8 0.7 copy-done.3
  12.4 3.5 %shard_map.69 = (bf16[1280,1280]{1,0:T(8,128)(2,1)S(1)}, bf16[1280,1280]{1,0:T(8,128)(2,1)S(1)}, s32[28]{0:T(128)S(1)}) custom-call(s32[80]{0:T(128)S(1)} %copy-done.3, s32[2,40]{1,0:T(2,128)S(1)} %copy-done.2, f32[1280,1280]{1,0:T(8,128)} %a_hbm.1), custom_call_target="tpu_custom_call" | custom-call | flops 6553600 | bytes 13107200 | tf_op jit(solution)/shard_map/pallas_call | solution.py:191
  16.0 0.0 collective-permute-done
  16.0 0.1 collective-permute-start.1
  16.1 1.2 %collective-permute-done.1 = f32[80,256]{1,0:T(8,128)S(1)} collective-permute-done((f32[80,256]{1,0:T(8,128)S(1)}, f32[80,256]{1,0:T(8,128)S(1)}, u32[]{:S(2)}, u32[]{:S(2)}) %collective-permute-start.1) | collective-permute-done | bytes 81952 | tf_op jit(solution)/shard_map/ppermute | solution.py:210
  17.4 3.3 %collective-permute-start.3 = (f32[160,256]{1,0:T(8,128)S(1)}, f32[160,256]{1,0:T(8,128)S(1)}, u32[]{:S(2)}, u32[]{:S(2)}) collective-permute-start(f32[160,256]{1,0:T(8,128)S(1)} %constant_dynamic-update-slice_fusion.refs_0_), channel_id=1, source_target_pairs={{0,64},{16,208},{32,96},{48,240},{64,128},{80,16},{96,160},{112,48... | collective-permute-start | bytes 491528 | tf_op jit(solution)/shard_map/ppermute | solution.py:208
  20.7 1.9 %collective-permute-start.2 = (f32[160,256]{1,0:T(8,128)S(1)}, f32[160,256]{1,0:T(8,128)S(1)}, u32[]{:S(2)}, u32[]{:S(2)}) collective-permute-start(f32[160,256]{1,0:T(8,128)S(1)} %constant_dynamic-update-slice_fusion.refs_0_), channel_id=1, source_target_pairs={{0,32},{16,240},{32,64},{48,16},{64,96},{80,48},{96,128},{112,80},... | collective-permute-start | bytes 491528 | tf_op jit(solution)/shard_map/ppermute | solution.py:208
  22.6 1.9 %collective-permute-done.3.refs_2_ = f32[160,256]{1,0:T(8,128)S(1)} collective-permute-done((f32[160,256]{1,0:T(8,128)S(1)}, f32[160,256]{1,0:T(8,128)S(1)}, u32[]{:S(2)}, u32[]{:S(2)}) %collective-permute-start.3) | collective-permute-done | bytes 163872 | tf_op jit(solution)/shard_map/ppermute | solution.py:208
  24.6 3.2 %collective-permute-start.4 = (f32[160,256]{1,0:T(8,128)S(1)}, f32[160,256]{1,0:T(8,128)S(1)}, u32[]{:S(2)}, u32[]{:S(2)}) collective-permute-start(f32[160,256]{1,0:T(8,128)S(1)} %collective-permute-done.3.refs_2_), channel_id=1, source_target_pairs={{0,32},{16,240},{32,64},{48,16},{64,96},{80,48},{96,128},{112,80},... | collective-permute-start | bytes 491528 | tf_op jit(solution)/shard_map/ppermute | solution.py:208
  27.7 0.0 copy-start
  27.7 2.0 %collective-permute-start.5 = (f32[80,256]{1,0:T(8,128)S(1)}, f32[80,256]{1,0:T(8,128)S(1)}, u32[]{:S(2)}, u32[]{:S(2)}) collective-permute-start(f32[80,256]{1,0:T(8,128)S(1)} %slice.4), channel_id=1, source_target_pairs={{0,64},{16,208},{32,96},{48,240},{64,128},{80,16},{96,160},{112,48... | collective-permute-start | bytes 245768 | tf_op jit(solution)/shard_map/ppermute | solution.py:208
  29.7 0.0 collective-permute-start.7
  29.7 0.0 collective-permute-done.2.refs_1_
  29.7 0.5 collective-permute-start.6
  30.2 0.0 collective-permute-done.4.refs_3_
  30.2 2.5 %collective-permute-start.8 = (f32[160,256]{1,0:T(8,128)S(1)}, f32[160,256]{1,0:T(8,128)S(1)}, u32[]{:S(2)}, u32[]{:S(2)}) collective-permute-start(f32[160,256]{1,0:T(8,128)S(1)} %collective-permute-done.4.refs_3_), channel_id=1, source_target_pairs={{0,16},{16,0},{32,48},{48,32},{64,80},{80,64},{96,112},{112,96},{1... | collective-permute-start | bytes 491528 | tf_op jit(solution)/shard_map/ppermute | solution.py:214
  32.7 0.2 collective-permute-done.5.refs_4_
  32.9 3.0 %collective-permute-start.9 = (f32[80,256]{1,0:T(8,128)S(1)}, f32[80,256]{1,0:T(8,128)S(1)}, u32[]{:S(2)}, u32[]{:S(2)}) collective-permute-start(f32[80,256]{1,0:T(8,128)S(1)} %collective-permute-done.5.refs_4_), channel_id=1, source_target_pairs={{0,16},{16,0},{32,48},{48,32},{64,80},{80,64},{96,112},{112,96},{1... | collective-permute-start | bytes 245768 | tf_op jit(solution)/shard_map/ppermute | solution.py:214
  35.9 0.9 collective-permute-done.9.refs_8_
  36.8 0.0 collective-permute-done.7.refs_6_
  36.9 0.0 collective-permute-done.6.refs_5_
  36.9 0.0 collective-permute-done.8.refs_7_
  36.9 3.8 %shard_map.70 = f32[1280,256]{1,0:T(8,128)S(1)} custom-call(s32[28]{0:T(128)S(1)} %get-tuple-element.18.sets_ref, bf16[1280,1280]{1,0:T(8,128)(2,1)S(1)} %get-tuple-element.19.high_ref, bf16[1280,1280]{1,0:T(8,128)(2,1)S(1)} %get-tuple-element.20.low_ref, f32[160,256]{1,0:T(8,128)S(1)} %constant_dynamic-update-slice_fusion.refs_0_, ...), custom_call_target="tpu_custom_call" | custom-call | flops 2516582400 | bytes 9175040 | tf_op jit(solution)/shard_map/pallas_call | solution.py:216
  40.6 0.0 copy-start.1
  40.7 24.5 %all_to_all.20.parts_ref = f32[16,80,256]{2,1,0:T(8,128)S(1)} all-to-all(f32[16,80,256]{2,1,0:T(8,128)S(1)} %bitcast.3), channel_id=1, replica_groups=mesh['prow'=16,'pcol'=16] {'pcol'}, dimensions={0} | all-to-all | bytes 2621440 | tf_op jit(solution)/shard_map/all_to_all | solution.py:227
  65.2 0.0 copy-done
  65.2 0.9 shard_map.71
  66.0 1.5 %collective-permute-start.10 = (f32[256,256]{1,0:T(8,128)S(1)}, f32[256,256]{1,0:T(8,128)S(1)}, u32[]{:S(2)}, u32[]{:S(2)}) collective-permute-start(f32[256,256]{1,0:T(8,128)S(1)} %get-tuple-element.23), channel_id=1, source_target_pairs={{0,16},{16,0},{32,48},{48,32},{64,80},{80,64},{96,112},{112,96},{1... | collective-permute-start | bytes 786440 | tf_op jit(solution)/shard_map/ppermute | solution.py:247
  67.6 0.8 shard_map.72
  68.4 0.3 collective-permute-done.10
  68.8 10.7 %all_to_all.21 = f32[16,16,256]{2,1,0:T(8,128)S(1)} all-to-all(f32[16,16,256]{2,1,0:T(8,128)S(1)} %bitcast.6), channel_id=1, replica_groups=mesh['prow'=16,'pcol'=16] {'pcol'}, dimensions={0} | all-to-all | bytes 524288 | tf_op jit(solution)/shard_map/all_to_all | solution.py:248
  79.6 13.2 %all_to_all.22 = f32[8,16,256]{2,1,0:T(8,128)S(1)} all-to-all(f32[8,16,256]{2,1,0:T(8,128)S(1)} %broadcast_in_dim.4), channel_id=1, replica_groups={{0,32,64,96,128,160,192,224},{16,48,80,112,144,176,208,240},{1,33,65,97..., dimensions={0} | all-to-all | bytes 262144 | tf_op jit(solution)/shard_map/all_to_all | solution.py:250
  92.8 10.1 %all_to_all.23 = f32[16,16,256]{2,1,0:T(8,128)S(1)} all-to-all(f32[16,16,256]{2,1,0:T(8,128)S(1)} %broadcast_in_dim.5), channel_id=1, replica_groups=mesh['prow'=16,'pcol'=16] {'pcol'}, dimensions={0} | all-to-all | bytes 524288 | tf_op jit(solution)/shard_map/all_to_all | solution.py:252
  103.0 4.4 %collective-permute-start.11 = (f32[256,256]{1,0:T(8,128)S(1)}, f32[256,256]{1,0:T(8,128)S(1)}, u32[]{:S(2)}, u32[]{:S(2)}) collective-permute-start(f32[256,256]{1,0:T(8,128)S(1)} %bitcast.4), channel_id=1, source_target_pairs={{0,16},{16,0},{32,48},{48,32},{64,80},{80,64},{96,112},{112,96},{1... | collective-permute-start | bytes 786440 | tf_op jit(solution)/shard_map/ppermute | solution.py:253
  107.4 1.2 %shard_map.73 = f32[80,512]{1,0:T(8,128)} custom-call(s32[28]{0:T(128)S(1)} %get-tuple-element.18.sets_ref, f32[80,256]{1,0:T(8,128)S(1)} %get-tuple-element.24.y_ref), custom_call_target="tpu_custom_call" | custom-call | tf_op jit(solution)/shard_map/pallas_call | solution.py:255
  108.6 0.0 collective-permute-done.11.there_ref
  108.6 0.0 copy-done.1
  108.6 0.9 shard_map.74
  (8 shorter events, 0.1 us)
Async XLA Ops:
  2.2 13.8 %collective-permute-start = (f32[80,256]{1,0:T(8,128)}, f32[80,256]{1,0:T(8,128)S(1)}, u32[]{:S(2)}, u32[]{:S(2)}) collective-permute-start(f32[80,256]{1,0:T(8,128)} %shard_map.68.z_ref), channel_id=1, source_target_pairs={{10,0},{6,16},{9,32},{11,48},{5,64},{7,80},{15,96},{1,112},{12,128... | collective-permute-start | bytes 245768 | tf_op jit(solution)/shard_map/ppermute | solution.py:190
  11.1 0.7 copy-start.2
  11.8 0.7 copy-start.3
  16.0 1.4 %collective-permute-start.1 = (f32[80,256]{1,0:T(8,128)S(1)}, f32[80,256]{1,0:T(8,128)S(1)}, u32[]{:S(2)}, u32[]{:S(2)}) collective-permute-start(f32[80,256]{1,0:T(8,128)S(1)} %collective-permute-done), channel_id=1, source_target_pairs={{0,16},{16,0},{32,48},{48,32},{64,80},{80,64},{96,112},{112,96},{1... | collective-permute-start | bytes 245768 | tf_op jit(solution)/shard_map/ppermute | solution.py:210
  17.4 7.2 %collective-permute-start.3 = (f32[160,256]{1,0:T(8,128)S(1)}, f32[160,256]{1,0:T(8,128)S(1)}, u32[]{:S(2)}, u32[]{:S(2)}) collective-permute-start(f32[160,256]{1,0:T(8,128)S(1)} %constant_dynamic-update-slice_fusion.refs_0_), channel_id=1, source_target_pairs={{0,64},{16,208},{32,96},{48,240},{64,128},{80,16},{96,160},{112,48... | collective-permute-start | bytes 491528 | tf_op jit(solution)/shard_map/ppermute | solution.py:208
  20.7 9.0 %collective-permute-start.2 = (f32[160,256]{1,0:T(8,128)S(1)}, f32[160,256]{1,0:T(8,128)S(1)}, u32[]{:S(2)}, u32[]{:S(2)}) collective-permute-start(f32[160,256]{1,0:T(8,128)S(1)} %constant_dynamic-update-slice_fusion.refs_0_), channel_id=1, source_target_pairs={{0,32},{16,240},{32,64},{48,16},{64,96},{80,48},{96,128},{112,80},... | collective-permute-start | bytes 491528 | tf_op jit(solution)/shard_map/ppermute | solution.py:208
  24.6 5.7 %collective-permute-start.4 = (f32[160,256]{1,0:T(8,128)S(1)}, f32[160,256]{1,0:T(8,128)S(1)}, u32[]{:S(2)}, u32[]{:S(2)}) collective-permute-start(f32[160,256]{1,0:T(8,128)S(1)} %collective-permute-done.3.refs_2_), channel_id=1, source_target_pairs={{0,32},{16,240},{32,64},{48,16},{64,96},{80,48},{96,128},{112,80},... | collective-permute-start | bytes 491528 | tf_op jit(solution)/shard_map/ppermute | solution.py:208
  27.7 37.5 %copy-start = (f32[80,256]{1,0:T(8,128)S(1)}, f32[80,256]{1,0:T(8,128)}, u32[]{:S(2)}) copy-start(f32[80,256]{1,0:T(8,128)} %shard_map.68.z_ref) | copy-start | bytes 245764
  27.7 5.1 %collective-permute-start.5 = (f32[80,256]{1,0:T(8,128)S(1)}, f32[80,256]{1,0:T(8,128)S(1)}, u32[]{:S(2)}, u32[]{:S(2)}) collective-permute-start(f32[80,256]{1,0:T(8,128)S(1)} %slice.4), channel_id=1, source_target_pairs={{0,64},{16,208},{32,96},{48,240},{64,128},{80,16},{96,160},{112,48... | collective-permute-start | bytes 245768 | tf_op jit(solution)/shard_map/ppermute | solution.py:208
  29.7 7.1 %collective-permute-start.7 = (f32[160,256]{1,0:T(8,128)S(1)}, f32[160,256]{1,0:T(8,128)S(1)}, u32[]{:S(2)}, u32[]{:S(2)}) collective-permute-start(f32[160,256]{1,0:T(8,128)S(1)} %collective-permute-done.3.refs_2_), channel_id=1, source_target_pairs={{0,16},{16,0},{32,48},{48,32},{64,80},{80,64},{96,112},{112,96},{1... | collective-permute-start | bytes 491528 | tf_op jit(solution)/shard_map/ppermute | solution.py:214
  29.7 7.1 %collective-permute-start.6 = (f32[160,256]{1,0:T(8,128)S(1)}, f32[160,256]{1,0:T(8,128)S(1)}, u32[]{:S(2)}, u32[]{:S(2)}) collective-permute-start(f32[160,256]{1,0:T(8,128)S(1)} %collective-permute-done.2.refs_1_), channel_id=1, source_target_pairs={{0,16},{16,0},{32,48},{48,32},{64,80},{80,64},{96,112},{112,96},{1... | collective-permute-start | bytes 491528 | tf_op jit(solution)/shard_map/ppermute | solution.py:214
  30.2 6.6 %collective-permute-start.8 = (f32[160,256]{1,0:T(8,128)S(1)}, f32[160,256]{1,0:T(8,128)S(1)}, u32[]{:S(2)}, u32[]{:S(2)}) collective-permute-start(f32[160,256]{1,0:T(8,128)S(1)} %collective-permute-done.4.refs_3_), channel_id=1, source_target_pairs={{0,16},{16,0},{32,48},{48,32},{64,80},{80,64},{96,112},{112,96},{1... | collective-permute-start | bytes 491528 | tf_op jit(solution)/shard_map/ppermute | solution.py:214
  32.9 4.0 %collective-permute-start.9 = (f32[80,256]{1,0:T(8,128)S(1)}, f32[80,256]{1,0:T(8,128)S(1)}, u32[]{:S(2)}, u32[]{:S(2)}) collective-permute-start(f32[80,256]{1,0:T(8,128)S(1)} %collective-permute-done.5.refs_4_), channel_id=1, source_target_pairs={{0,16},{16,0},{32,48},{48,32},{64,80},{80,64},{96,112},{112,96},{1... | collective-permute-start | bytes 245768 | tf_op jit(solution)/shard_map/ppermute | solution.py:214
  40.6 68.0 %copy-start.1 = (f32[2,256,256]{2,1,0:T(8,128)S(1)}, f32[2,256,256]{2,1,0:T(8,128)}, u32[]{:S(2)}) copy-start(f32[2,256,256]{2,1,0:T(8,128)} %d_ref.1) | copy-start | bytes 1572868
  66.0 2.7 %collective-permute-start.10 = (f32[256,256]{1,0:T(8,128)S(1)}, f32[256,256]{1,0:T(8,128)S(1)}, u32[]{:S(2)}, u32[]{:S(2)}) collective-permute-start(f32[256,256]{1,0:T(8,128)S(1)} %get-tuple-element.23), channel_id=1, source_target_pairs={{0,16},{16,0},{32,48},{48,32},{64,80},{80,64},{96,112},{112,96},{1... | collective-permute-start | bytes 786440 | tf_op jit(solution)/shard_map/ppermute | solution.py:247
  103.0 5.6 %collective-permute-start.11 = (f32[256,256]{1,0:T(8,128)S(1)}, f32[256,256]{1,0:T(8,128)S(1)}, u32[]{:S(2)}, u32[]{:S(2)}) collective-permute-start(f32[256,256]{1,0:T(8,128)S(1)} %bitcast.4), channel_id=1, source_target_pairs={{0,16},{16,0},{32,48},{48,32},{64,80},{80,64},{96,112},{112,96},{1... | collective-permute-start | bytes 786440 | tf_op jit(solution)/shard_map/ppermute | solution.py:253

commit v5 on v4

--- a/solution.py
+++ b/solution.py
@@ -102,7 +102,7 @@
     n_blocks = high_ref.shape[0] // block
     row = lax.axis_index(ROW)
     core = row % 2
-    steps = [0, 1, 2, 3, 4, 1, 2, 3, 4]
+    steps = [0, 1, 2, 3, 4, 1, 2, 3]
     for n, (source, step) in enumerate(zip(sources, steps)):
         owner = core if n < 5 else 1 - core
         z = (row // 2 + n_z + step * (2 * owner - 1)) % n_z
@@ -209,9 +209,9 @@
 
     chunk = jnp.concatenate([turned, lax.ppermute(turned, ROW, swap)])
     one, two = along(chunk, 1), along(chunk, 2)
-    three, four = along(two, 1), along(two[:rows_dev], 2)
-    pieces = [one, two, three, four]
-    pieces = [chunk, *pieces, *(lax.ppermute(p, ROW, swap) for p in pieces)]
+    three, four = along(two, 1), along(two, 2)
+    pieces = [one, two, three]
+    pieces = [chunk, *pieces, four, *(lax.ppermute(p, ROW, swap) for p in pieces)]
 
     sent = pl.pallas_call(
         functools.partial(product_kernel, block, rows_dev, n_z),

time: 110 us -> 110 us (level)
    ppermute x4 -> x3, starting transfers between devices: 6.02 us -> 2.68 us  [per_device(): lax.ppermute(p, ROW, swap)]
    ppermute x1, starting transfers between devices: 1.55 us -> 4.52 us  [per_device(): terms = keep + lax.ppermute(send, ROW, swap)]
    all_to_all x1, blocking collectives: 13.2 us -> 15.6 us  [per_device(): lax.all_to_all(terms, ROW, 0, 0, axis_index_groups=groups)]
    all_to_all x1, blocking collectives: 24.5 us -> 22.2 us  [per_device(): parts = lax.all_to_all(sent.reshape(n_col, rows_dev, block), COL, 0, 0)]
  transfers between devices with their start and end apart: 12 -> 11, of which waited for: 5 -> 5; matrix products, arithmetic and copies ran while one was open for 0% -> 0% of each run, Pallas kernels for 5% -> 5%
where the time goes in v5:
time: 110 us; the launch traced here: 109 us
  blocking collectives  58.7 us (53%)
  starting transfers between devices  31.4 us (29%)
  Pallas kernels  12.7 us (12%)
  waiting for transfers between devices  4.45 us (4%)
  local copies, waits for them, and re-layouts  1.39 us (1%)
    all_to_all x1, blocking collectives, per_device(): parts = lax.all_to_all(sent.reshape(n_col, rows_dev, block), COL, 0, 0)  22.2 us
    all_to_all x1, blocking collectives, per_device(): lax.all_to_all(terms, ROW, 0, 0, axis_index_groups=groups)  15.6 us
    ppermute x4, starting transfers between devices, along(): return lax.ppermute(x, ROW, pairs)  10.8 us
    all_to_all x1, blocking collectives, per_device(): lax.all_to_all(terms.reshape(n_col, per, block), COL, 0, 0)  10.8 us
    all_to_all x1, blocking collectives, per_device(): here = lax.all_to_all(terms, COL, 0, 0).reshape(block, block)  10.1 us
    ppermute x1, starting transfers between devices, per_device(): lax.ppermute(z, (ROW, COL), [(j * n_col + s, p * n_col + j) for (j, s), p...  8.87 us
    ppermute x1, starting transfers between devices, per_device(): terms = keep + lax.ppermute(send, ROW, swap)  4.52 us
    ppermute x1, starting transfers between devices, per_device(): there = lax.ppermute(here, ROW, swap)  4.4 us
  transfers between devices with their start and end apart: 11, of which 5 were waited for; matrix products, arithmetic and copies ran while one was open for 0% of the time, Pallas kernels for 5%

profile of v5, /device:TPU:1, one launch (start us, length us, event | category | flops | bytes accessed | tf_op | source)
XLA Modules:
  0.0 109.4 jit_solution(15795573374500615262)
XLA Ops:
  0.6 1.6 %shard_map.68.z_ref = f32[80,256]{1,0:T(8,128)} custom-call(s32[80]{0:T(128)} %owner_hbm.3, s32[2,40]{1,0:T(2,128)} %ancestors_hbm.3, f32[80,512]{1,0:T(8,128)} %panel_hbm.1), custom_call_target="tpu_custom_call" | custom-call | tf_op jit(solution)/shard_map/pallas_call | solution.py:177
  2.2 8.9 %collective-permute-start = (f32[80,256]{1,0:T(8,128)}, f32[80,256]{1,0:T(8,128)S(1)}, u32[]{:S(2)}, u32[]{:S(2)}) collective-permute-start(f32[80,256]{1,0:T(8,128)} %shard_map.68.z_ref), channel_id=1, source_target_pairs={{10,0},{6,16},{9,32},{11,48},{5,64},{7,80},{15,96},{1,112},{12,128... | collective-permute-start | bytes 245768 | tf_op jit(solution)/shard_map/ppermute | solution.py:190
  11.1 0.0 copy-start.2
  11.1 0.7 copy-done.2
  11.8 0.0 copy-start.3
  11.8 0.7 copy-done.3
  12.4 3.5 %shard_map.69 = (bf16[1280,1280]{1,0:T(8,128)(2,1)S(1)}, bf16[1280,1280]{1,0:T(8,128)(2,1)S(1)}, s32[28]{0:T(128)S(1)}) custom-call(s32[80]{0:T(128)S(1)} %copy-done.3, s32[2,40]{1,0:T(2,128)S(1)} %copy-done.2, f32[1280,1280]{1,0:T(8,128)} %a_hbm.1), custom_call_target="tpu_custom_call" | custom-call | flops 6553600 | bytes 13107200 | tf_op jit(solution)/shard_map/pallas_call | solution.py:191
  16.0 0.0 collective-permute-done
  16.0 0.1 collective-permute-start.1
  16.1 1.2 %collective-permute-done.1 = f32[80,256]{1,0:T(8,128)S(1)} collective-permute-done((f32[80,256]{1,0:T(8,128)S(1)}, f32[80,256]{1,0:T(8,128)S(1)}, u32[]{:S(2)}, u32[]{:S(2)}) %collective-permute-start.1) | collective-permute-done | bytes 81952 | tf_op jit(solution)/shard_map/ppermute | solution.py:210
  17.4 0.0 copy-start
  17.4 3.3 %collective-permute-start.3 = (f32[160,256]{1,0:T(8,128)S(1)}, f32[160,256]{1,0:T(8,128)S(1)}, u32[]{:S(2)}, u32[]{:S(2)}) collective-permute-start(f32[160,256]{1,0:T(8,128)S(1)} %constant_dynamic-update-slice_fusion.refs_0_), channel_id=1, source_target_pairs={{0,64},{16,208},{32,96},{48,240},{64,128},{80,16},{96,160},{112,48... | collective-permute-start | bytes 491528 | tf_op jit(solution)/shard_map/ppermute | solution.py:208
  20.7 2.0 %collective-permute-start.2 = (f32[160,256]{1,0:T(8,128)S(1)}, f32[160,256]{1,0:T(8,128)S(1)}, u32[]{:S(2)}, u32[]{:S(2)}) collective-permute-start(f32[160,256]{1,0:T(8,128)S(1)} %constant_dynamic-update-slice_fusion.refs_0_), channel_id=1, source_target_pairs={{0,32},{16,240},{32,64},{48,16},{64,96},{80,48},{96,128},{112,80},... | collective-permute-start | bytes 491528 | tf_op jit(solution)/shard_map/ppermute | solution.py:208
  22.7 1.9 %collective-permute-done.3.refs_2_ = f32[160,256]{1,0:T(8,128)S(1)} collective-permute-done((f32[160,256]{1,0:T(8,128)S(1)}, f32[160,256]{1,0:T(8,128)S(1)}, u32[]{:S(2)}, u32[]{:S(2)}) %collective-permute-start.3) | collective-permute-done | bytes 163872 | tf_op jit(solution)/shard_map/ppermute | solution.py:208
  24.6 3.2 %collective-permute-start.4 = (f32[160,256]{1,0:T(8,128)S(1)}, f32[160,256]{1,0:T(8,128)S(1)}, u32[]{:S(2)}, u32[]{:S(2)}) collective-permute-start(f32[160,256]{1,0:T(8,128)S(1)} %collective-permute-done.3.refs_2_), channel_id=1, source_target_pairs={{0,32},{16,240},{32,64},{48,16},{64,96},{80,48},{96,128},{112,80},... | collective-permute-start | bytes 491528 | tf_op jit(solution)/shard_map/ppermute | solution.py:208
  27.8 0.6 collective-permute-start.7
  28.4 2.2 %collective-permute-start.5 = (f32[160,256]{1,0:T(8,128)S(1)}, f32[160,256]{1,0:T(8,128)S(1)}, u32[]{:S(2)}, u32[]{:S(2)}) collective-permute-start(f32[160,256]{1,0:T(8,128)S(1)} %collective-permute-done.3.refs_2_), channel_id=1, source_target_pairs={{0,64},{16,208},{32,96},{48,240},{64,128},{80,16},{96,160},{112,48... | collective-permute-start | bytes 491528 | tf_op jit(solution)/shard_map/ppermute | solution.py:208
  30.6 0.0 collective-permute-done.2.refs_1_
  30.6 0.0 collective-permute-start.6
  30.6 0.0 collective-permute-done.4.refs_3_
  30.6 2.1 %collective-permute-start.8 = (f32[160,256]{1,0:T(8,128)S(1)}, f32[160,256]{1,0:T(8,128)S(1)}, u32[]{:S(2)}, u32[]{:S(2)}) collective-permute-start(f32[160,256]{1,0:T(8,128)S(1)} %collective-permute-done.4.refs_3_), channel_id=1, source_target_pairs={{0,16},{16,0},{32,48},{48,32},{64,80},{80,64},{96,112},{112,96},{1... | collective-permute-start | bytes 491528 | tf_op jit(solution)/shard_map/ppermute | solution.py:214
  32.7 0.0 collective-permute-done.7.refs_6_
  32.7 0.8 collective-permute-done.5.refs_4_
  33.5 0.0 collective-permute-done.6.refs_5_
  33.5 0.2 collective-permute-done.8.refs_7_
  33.8 3.8 %shard_map.70 = f32[1280,256]{1,0:T(8,128)S(1)} custom-call(s32[28]{0:T(128)S(1)} %get-tuple-element.18.sets_ref, bf16[1280,1280]{1,0:T(8,128)(2,1)S(1)} %get-tuple-element.19.high_ref, bf16[1280,1280]{1,0:T(8,128)(2,1)S(1)} %get-tuple-element.20.low_ref, f32[160,256]{1,0:T(8,128)S(1)} %constant_dynamic-update-slice_fusion.refs_0_, ...), custom_call_target="tpu_custom_call" | custom-call | flops 2516582400 | bytes 9175040 | tf_op jit(solution)/shard_map/pallas_call | solution.py:216
  37.5 0.0 copy-start.1
  37.5 22.2 %all_to_all.20.parts_ref = f32[16,80,256]{2,1,0:T(8,128)S(1)} all-to-all(f32[16,80,256]{2,1,0:T(8,128)S(1)} %bitcast.3), channel_id=1, replica_groups=mesh['prow'=16,'pcol'=16] {'pcol'}, dimensions={0} | all-to-all | bytes 2621440 | tf_op jit(solution)/shard_map/all_to_all | solution.py:227
  59.8 0.0 copy-done
  59.8 0.9 shard_map.71
  60.6 4.5 %collective-permute-start.9 = (f32[256,256]{1,0:T(8,128)S(1)}, f32[256,256]{1,0:T(8,128)S(1)}, u32[]{:S(2)}, u32[]{:S(2)}) collective-permute-start(f32[256,256]{1,0:T(8,128)S(1)} %get-tuple-element.23), channel_id=1, source_target_pairs={{0,16},{16,0},{32,48},{48,32},{64,80},{80,64},{96,112},{112,96},{1... | collective-permute-start | bytes 786440 | tf_op jit(solution)/shard_map/ppermute | solution.py:247
  65.1 0.8 shard_map.72
  66.0 0.3 collective-permute-done.9
  66.3 10.8 %all_to_all.21 = f32[16,16,256]{2,1,0:T(8,128)S(1)} all-to-all(f32[16,16,256]{2,1,0:T(8,128)S(1)} %bitcast.6), channel_id=1, replica_groups=mesh['prow'=16,'pcol'=16] {'pcol'}, dimensions={0} | all-to-all | bytes 524288 | tf_op jit(solution)/shard_map/all_to_all | solution.py:248
  77.2 15.6 %all_to_all.22 = f32[8,16,256]{2,1,0:T(8,128)S(1)} all-to-all(f32[8,16,256]{2,1,0:T(8,128)S(1)} %broadcast_in_dim.4), channel_id=1, replica_groups={{0,32,64,96,128,160,192,224},{16,48,80,112,144,176,208,240},{1,33,65,97..., dimensions={0} | all-to-all | bytes 262144 | tf_op jit(solution)/shard_map/all_to_all | solution.py:250
  92.8 10.1 %all_to_all.23 = f32[16,16,256]{2,1,0:T(8,128)S(1)} all-to-all(f32[16,16,256]{2,1,0:T(8,128)S(1)} %broadcast_in_dim.5), channel_id=1, replica_groups=mesh['prow'=16,'pcol'=16] {'pcol'}, dimensions={0} | all-to-all | bytes 524288 | tf_op jit(solution)/shard_map/all_to_all | solution.py:252
  102.9 4.4 %collective-permute-start.10 = (f32[256,256]{1,0:T(8,128)S(1)}, f32[256,256]{1,0:T(8,128)S(1)}, u32[]{:S(2)}, u32[]{:S(2)}) collective-permute-start(f32[256,256]{1,0:T(8,128)S(1)} %bitcast.4), channel_id=1, source_target_pairs={{0,16},{16,0},{32,48},{48,32},{64,80},{80,64},{96,112},{112,96},{1... | collective-permute-start | bytes 786440 | tf_op jit(solution)/shard_map/ppermute | solution.py:253
  107.3 1.2 %shard_map.73 = f32[80,512]{1,0:T(8,128)} custom-call(s32[28]{0:T(128)S(1)} %get-tuple-element.18.sets_ref, f32[80,256]{1,0:T(8,128)S(1)} %get-tuple-element.24.y_ref), custom_call_target="tpu_custom_call" | custom-call | tf_op jit(solution)/shard_map/pallas_call | solution.py:255
  108.5 0.0 collective-permute-done.10.there_ref
  108.5 0.0 copy-done.1
  108.5 0.9 shard_map.74
  (7 shorter events, 0.1 us)
Async XLA Ops:
  2.2 13.8 %collective-permute-start = (f32[80,256]{1,0:T(8,128)}, f32[80,256]{1,0:T(8,128)S(1)}, u32[]{:S(2)}, u32[]{:S(2)}) collective-permute-start(f32[80,256]{1,0:T(8,128)} %shard_map.68.z_ref), channel_id=1, source_target_pairs={{10,0},{6,16},{9,32},{11,48},{5,64},{7,80},{15,96},{1,112},{12,128... | collective-permute-start | bytes 245768 | tf_op jit(solution)/shard_map/ppermute | solution.py:190
  11.1 0.7 copy-start.2
  11.8 0.7 copy-start.3
  16.0 1.4 %collective-permute-start.1 = (f32[80,256]{1,0:T(8,128)S(1)}, f32[80,256]{1,0:T(8,128)S(1)}, u32[]{:S(2)}, u32[]{:S(2)}) collective-permute-start(f32[80,256]{1,0:T(8,128)S(1)} %collective-permute-done), channel_id=1, source_target_pairs={{0,16},{16,0},{32,48},{48,32},{64,80},{80,64},{96,112},{112,96},{1... | collective-permute-start | bytes 245768 | tf_op jit(solution)/shard_map/ppermute | solution.py:210
  17.4 42.4 %copy-start = (f32[80,256]{1,0:T(8,128)S(1)}, f32[80,256]{1,0:T(8,128)}, u32[]{:S(2)}) copy-start(f32[80,256]{1,0:T(8,128)} %shard_map.68.z_ref) | copy-start | bytes 245764
  17.4 7.2 %collective-permute-start.3 = (f32[160,256]{1,0:T(8,128)S(1)}, f32[160,256]{1,0:T(8,128)S(1)}, u32[]{:S(2)}, u32[]{:S(2)}) collective-permute-start(f32[160,256]{1,0:T(8,128)S(1)} %constant_dynamic-update-slice_fusion.refs_0_), channel_id=1, source_target_pairs={{0,64},{16,208},{32,96},{48,240},{64,128},{80,16},{96,160},{112,48... | collective-permute-start | bytes 491528 | tf_op jit(solution)/shard_map/ppermute | solution.py:208
  20.7 9.9 %collective-permute-start.2 = (f32[160,256]{1,0:T(8,128)S(1)}, f32[160,256]{1,0:T(8,128)S(1)}, u32[]{:S(2)}, u32[]{:S(2)}) collective-permute-start(f32[160,256]{1,0:T(8,128)S(1)} %constant_dynamic-update-slice_fusion.refs_0_), channel_id=1, source_target_pairs={{0,32},{16,240},{32,64},{48,16},{64,96},{80,48},{96,128},{112,80},... | collective-permute-start | bytes 491528 | tf_op jit(solution)/shard_map/ppermute | solution.py:208
  24.6 6.0 %collective-permute-start.4 = (f32[160,256]{1,0:T(8,128)S(1)}, f32[160,256]{1,0:T(8,128)S(1)}, u32[]{:S(2)}, u32[]{:S(2)}) collective-permute-start(f32[160,256]{1,0:T(8,128)S(1)} %collective-permute-done.3.refs_2_), channel_id=1, source_target_pairs={{0,32},{16,240},{32,64},{48,16},{64,96},{80,48},{96,128},{112,80},... | collective-permute-start | bytes 491528 | tf_op jit(solution)/shard_map/ppermute | solution.py:208
  27.8 4.9 %collective-permute-start.7 = (f32[160,256]{1,0:T(8,128)S(1)}, f32[160,256]{1,0:T(8,128)S(1)}, u32[]{:S(2)}, u32[]{:S(2)}) collective-permute-start(f32[160,256]{1,0:T(8,128)S(1)} %collective-permute-done.3.refs_2_), channel_id=1, source_target_pairs={{0,16},{16,0},{32,48},{48,32},{64,80},{80,64},{96,112},{112,96},{1... | collective-permute-start | bytes 491528 | tf_op jit(solution)/shard_map/ppermute | solution.py:214
  28.4 5.2 %collective-permute-start.5 = (f32[160,256]{1,0:T(8,128)S(1)}, f32[160,256]{1,0:T(8,128)S(1)}, u32[]{:S(2)}, u32[]{:S(2)}) collective-permute-start(f32[160,256]{1,0:T(8,128)S(1)} %collective-permute-done.3.refs_2_), channel_id=1, source_target_pairs={{0,64},{16,208},{32,96},{48,240},{64,128},{80,16},{96,160},{112,48... | collective-permute-start | bytes 491528 | tf_op jit(solution)/shard_map/ppermute | solution.py:208
  30.6 2.9 %collective-permute-start.6 = (f32[160,256]{1,0:T(8,128)S(1)}, f32[160,256]{1,0:T(8,128)S(1)}, u32[]{:S(2)}, u32[]{:S(2)}) collective-permute-start(f32[160,256]{1,0:T(8,128)S(1)} %collective-permute-done.2.refs_1_), channel_id=1, source_target_pairs={{0,16},{16,0},{32,48},{48,32},{64,80},{80,64},{96,112},{112,96},{1... | collective-permute-start | bytes 491528 | tf_op jit(solution)/shard_map/ppermute | solution.py:214
  30.6 3.1 %collective-permute-start.8 = (f32[160,256]{1,0:T(8,128)S(1)}, f32[160,256]{1,0:T(8,128)S(1)}, u32[]{:S(2)}, u32[]{:S(2)}) collective-permute-start(f32[160,256]{1,0:T(8,128)S(1)} %collective-permute-done.4.refs_3_), channel_id=1, source_target_pairs={{0,16},{16,0},{32,48},{48,32},{64,80},{80,64},{96,112},{112,96},{1... | collective-permute-start | bytes 491528 | tf_op jit(solution)/shard_map/ppermute | solution.py:214
  37.5 71.0 %copy-start.1 = (f32[2,256,256]{2,1,0:T(8,128)S(1)}, f32[2,256,256]{2,1,0:T(8,128)}, u32[]{:S(2)}) copy-start(f32[2,256,256]{2,1,0:T(8,128)} %d_ref.1) | copy-start | bytes 1572868
  60.6 5.7 %collective-permute-start.9 = (f32[256,256]{1,0:T(8,128)S(1)}, f32[256,256]{1,0:T(8,128)S(1)}, u32[]{:S(2)}, u32[]{:S(2)}) collective-permute-start(f32[256,256]{1,0:T(8,128)S(1)} %get-tuple-element.23), channel_id=1, source_target_pairs={{0,16},{16,0},{32,48},{48,32},{64,80},{80,64},{96,112},{112,96},{1... | collective-permute-start | bytes 786440 | tf_op jit(solution)/shard_map/ppermute | solution.py:247
  102.9 5.6 %collective-permute-start.10 = (f32[256,256]{1,0:T(8,128)S(1)}, f32[256,256]{1,0:T(8,128)S(1)}, u32[]{:S(2)}, u32[]{:S(2)}) collective-permute-start(f32[256,256]{1,0:T(8,128)S(1)} %bitcast.4), channel_id=1, source_target_pairs={{0,16},{16,0},{32,48},{48,32},{64,80},{80,64},{96,112},{112,96},{1... | collective-permute-start | bytes 786440 | tf_op jit(solution)/shard_map/ppermute | solution.py:253

commit v6 on v5

--- a/solution.py
+++ b/solution.py
@@ -97,17 +97,16 @@
         high_ref[rows, :], low_ref[rows, :] = split(a_ref[rows, :])
 
 
-def product_kernel(block, piece, n_z, sets_ref, high_ref, low_ref, *refs):
+def product_kernel(block, piece, n_z, places, sets_ref, high_ref, low_ref, *refs):
     *sources, out_ref, w_ref = refs
     n_blocks = high_ref.shape[0] // block
     row = lax.axis_index(ROW)
     core = row % 2
-    steps = [0, 1, 2, 3, 4, 1, 2, 3]
-    for n, (source, step) in enumerate(zip(sources, steps)):
-        owner = core if n < 5 else 1 - core
-        z = (row // 2 + n_z + step * (2 * owner - 1)) % n_z
-        for h in range(source.shape[0] // piece):
-            start = sets_ref[2 * n_blocks + 2 + 2 * z + (owner ^ h)] * piece
+    for source, (theirs, held) in zip(sources, places):
+        owner = 1 - core if theirs else core
+        for h, (step, which) in enumerate(held):
+            z = (row // 2 + n_z + step * (2 * owner - 1)) % n_z
+            start = sets_ref[2 * n_blocks + 2 + 2 * z + (owner ^ which)] * piece
             rows = pl.ds(pl.multiple_of(start, 16), piece)
             in_first = sets_ref[n_blocks + start // block]
             in_last = sets_ref[n_blocks + (start + piece - 1) // block]
@@ -207,14 +206,18 @@
         pairs = [(2 * q + c, 2 * ((q + step * (1 - 2 * c)) % n_z) + c) for q in range(n_z) for c in range(2)]
         return lax.ppermute(x, ROW, pairs)
 
-    chunk = jnp.concatenate([turned, lax.ppermute(turned, ROW, swap)])
-    one, two = along(chunk, 1), along(chunk, 2)
-    three, four = along(two, 1), along(two, 2)
-    pieces = [one, two, three]
-    pieces = [chunk, *pieces, four, *(lax.ppermute(p, ROW, swap) for p in pieces)]
+    other = lax.ppermute(turned, ROW, swap)
+    two, two_other = along(turned, 2), along(other, 2)
+    four = along(two, 2)
+    chunk, two = lax.optimization_barrier((jnp.concatenate([turned, other]), two))
+    one, three = along(chunk, 1), along(jnp.concatenate([two, two_other]), 1)
+    held = [[(1, 0), (1, 1)], [(2, 0)], [(2, 1)], [(3, 0), (3, 1)], [(4, 0)]]
+    pieces = [one, two, two_other, three, four]
+    places = [(0, [(0, 0)]), (0, [(0, 1)])] + [(theirs, h) for theirs in (0, 1) for h in held]
+    pieces = [turned, other, *pieces, *(lax.ppermute(p, ROW, swap) for p in pieces)]
 
     sent = pl.pallas_call(
-        functools.partial(product_kernel, block, rows_dev, n_z),
+        functools.partial(product_kernel, block, rows_dev, n_z, places),
         out_shape=jax.ShapeDtypeStruct((edge, block), f32),
         in_specs=[smem, vmem, vmem] + [vmem] * len(pieces),
         out_specs=vmem,

time: 110 us -> 109 us (level)
  waiting for transfers between devices: 4.45 us -> 2.03 us
  starting transfers between devices: 31.4 us -> 33.6 us
    ppermute x3 -> x5, starting transfers between devices: 2.68 us -> 6.04 us  [per_device(): lax.ppermute(p, ROW, swap)]
    ppermute x1, starting transfers between devices: 4.52 us -> 1.37 us  [per_device(): terms = keep + lax.ppermute(send, ROW, swap)]
    all_to_all x1, blocking collectives: 15.6 us -> 12.7 us  [per_device(): lax.all_to_all(terms, ROW, 0, 0, axis_index_groups=groups)]
    all_to_all x1, blocking collectives: 22.2 us -> 24.9 us  [per_device(): parts = lax.all_to_all(sent.reshape(n_col, rows_dev, block), COL, 0, 0)]
    ppermute x4 -> x5, waiting for transfers between devices: 2.68 us -> 0.44 us  [along(): return lax.ppermute(x, ROW, pairs)]
    ppermute x4 -> x5, starting transfers between devices: 10.8 us -> 12.9 us  [along(): return lax.ppermute(x, ROW, pairs)]
    ppermute x1, waiting for transfers between devices: 1.25 us -> 0.01 us  [per_device(): other = lax.ppermute(turned, ROW, swap)]
  transfers between devices with their start and end apart: 11 -> 14, of which waited for: 5 -> 4; matrix products, arithmetic and copies ran while one was open for 0% -> 0% of each run, Pallas kernels for 5% -> 5%
where the time goes in v6:
time: 109 us
  blocking collectives  58.6 us (54%)
  starting transfers between devices  33.6 us (31%)
  Pallas kernels  12.7 us (12%)
  waiting for transfers between devices  2.03 us (2%)
  local copies, waits for them, and re-layouts  1.38 us (1%)
    all_to_all x1, blocking collectives, per_device(): parts = lax.all_to_all(sent.reshape(n_col, rows_dev, block), COL, 0, 0)  24.9 us
    ppermute x5, starting transfers between devices, along(): return lax.ppermute(x, ROW, pairs)  12.9 us
    all_to_all x1, blocking collectives, per_device(): lax.all_to_all(terms, ROW, 0, 0, axis_index_groups=groups)  12.7 us
    all_to_all x1, blocking collectives, per_device(): lax.all_to_all(terms.reshape(n_col, per, block), COL, 0, 0)  10.8 us
    all_to_all x1, blocking collectives, per_device(): here = lax.all_to_all(terms, COL, 0, 0).reshape(block, block)  10.1 us
    ppermute x1, starting transfers between devices, per_device(): lax.ppermute(z, (ROW, COL), [(j * n_col + s, p * n_col + j) for (j, s), p...  8.87 us
    ppermute x5, starting transfers between devices, per_device(): lax.ppermute(p, ROW, swap)  6.04 us
    ppermute x1, starting transfers between devices, per_device(): there = lax.ppermute(here, ROW, swap)  4.4 us
  transfers between devices with their start and end apart: 14, of which 4 were waited for; matrix products, arithmetic and copies ran while one was open for 0% of the time, Pallas kernels for 5%

profile of v6, /device:TPU:1, one launch (start us, length us, event | category | flops | bytes accessed | tf_op | source)
XLA Modules:
  0.0 109.2 jit_solution(12038863812096252377)
XLA Ops:
  0.6 1.6 %shard_map.68.z_ref = f32[80,256]{1,0:T(8,128)} custom-call(s32[80]{0:T(128)} %owner_hbm.3, s32[2,40]{1,0:T(2,128)} %ancestors_hbm.3, f32[80,512]{1,0:T(8,128)} %panel_hbm.1), custom_call_target="tpu_custom_call" | custom-call | tf_op jit(solution)/shard_map/pallas_call | solution.py:176
  2.2 8.9 %collective-permute-start = (f32[80,256]{1,0:T(8,128)}, f32[80,256]{1,0:T(8,128)S(1)}, u32[]{:S(2)}, u32[]{:S(2)}) collective-permute-start(f32[80,256]{1,0:T(8,128)} %shard_map.68.z_ref), channel_id=1, source_target_pairs={{10,0},{6,16},{9,32},{11,48},{5,64},{7,80},{15,96},{1,112},{12,128... | collective-permute-start | bytes 245768 | tf_op jit(solution)/shard_map/ppermute | solution.py:189
  11.1 0.0 copy-start.2
  11.1 0.7 copy-done.2
  11.8 0.0 copy-start.3
  11.8 0.7 copy-done.3
  12.4 3.5 %shard_map.69 = (bf16[1280,1280]{1,0:T(8,128)(2,1)S(1)}, bf16[1280,1280]{1,0:T(8,128)(2,1)S(1)}, s32[28]{0:T(128)S(1)}) custom-call(s32[80]{0:T(128)S(1)} %copy-done.3, s32[2,40]{1,0:T(2,128)S(1)} %copy-done.2, f32[1280,1280]{1,0:T(8,128)} %a_hbm.1), custom_call_target="tpu_custom_call" | custom-call | flops 6553600 | bytes 13107200 | tf_op jit(solution)/shard_map/pallas_call | solution.py:190
  16.0 0.0 collective-permute-done.refs_0_
  16.0 0.1 collective-permute-start.1
  16.1 3.4 %collective-permute-start.2 = (f32[80,256]{1,0:T(8,128)S(1)}, f32[80,256]{1,0:T(8,128)S(1)}, u32[]{:S(2)}, u32[]{:S(2)}) collective-permute-start(f32[80,256]{1,0:T(8,128)S(1)} %collective-permute-done.refs_0_), channel_id=1, source_target_pairs={{0,64},{16,208},{32,96},{48,240},{64,128},{80,16},{96,160},{112,48... | collective-permute-start | bytes 245768 | tf_op jit(solution)/shard_map/ppermute | solution.py:207
  19.5 0.0 collective-permute-done.1.refs_1_
  19.5 2.9 %collective-permute-start.4 = (f32[80,256]{1,0:T(8,128)S(1)}, f32[80,256]{1,0:T(8,128)S(1)}, u32[]{:S(2)}, u32[]{:S(2)}) collective-permute-start(f32[80,256]{1,0:T(8,128)S(1)} %collective-permute-done.1.refs_1_), channel_id=1, source_target_pairs={{0,64},{16,208},{32,96},{48,240},{64,128},{80,16},{96,160},{112,48... | collective-permute-start | bytes 245768 | tf_op jit(solution)/shard_map/ppermute | solution.py:207
  22.5 0.0 collective-permute-done.2.refs_3_
  22.5 3.9 %collective-permute-start.3 = (f32[160,256]{1,0:T(8,128)S(1)}, f32[160,256]{1,0:T(8,128)S(1)}, u32[]{:S(2)}, u32[]{:S(2)}) collective-permute-start(f32[160,256]{1,0:T(8,128)S(1)} %pad_maximum_fusion), channel_id=1, source_target_pairs={{0,32},{16,240},{32,64},{48,16},{64,96},{80,48},{96,128},{112,80},... | collective-permute-start | bytes 491528 | tf_op jit(solution)/shard_map/ppermute | solution.py:207
  26.4 0.0 collective-permute-done.4.refs_4_
  26.4 0.0 copy-start
  26.4 0.9 collective-permute-start.5
  27.4 1.7 %collective-permute-start.6 = (f32[80,256]{1,0:T(8,128)S(1)}, f32[80,256]{1,0:T(8,128)S(1)}, u32[]{:S(2)}, u32[]{:S(2)}) collective-permute-start(f32[80,256]{1,0:T(8,128)S(1)} %collective-permute-done.2.refs_3_), channel_id=1, source_target_pairs={{0,64},{16,208},{32,96},{48,240},{64,128},{80,16},{96,160},{112,48... | collective-permute-start | bytes 245768 | tf_op jit(solution)/shard_map/ppermute | solution.py:207
  29.0 0.0 collective-permute-done.3.refs_2_
  29.0 1.5 %collective-permute-start.7 = (f32[160,256]{1,0:T(8,128)S(1)}, f32[160,256]{1,0:T(8,128)S(1)}, u32[]{:S(2)}, u32[]{:S(2)}) collective-permute-start(f32[160,256]{1,0:T(8,128)S(1)} %collective-permute-done.3.refs_2_), channel_id=1, source_target_pairs={{0,16},{16,0},{32,48},{48,32},{64,80},{80,64},{96,112},{112,96},{1... | collective-permute-start | bytes 491528 | tf_op jit(solution)/shard_map/ppermute | solution.py:217
  30.5 0.4 collective-permute-done.5.refs_5_
  31.0 1.6 %collective-permute-start.10 = (f32[160,256]{1,0:T(8,128)S(1)}, f32[160,256]{1,0:T(8,128)S(1)}, u32[]{:S(2)}, u32[]{:S(2)}) collective-permute-start(f32[160,256]{1,0:T(8,128)S(1)} %collective-permute-done.5.refs_5_), channel_id=1, source_target_pairs={{0,16},{16,0},{32,48},{48,32},{64,80},{80,64},{96,112},{112,96},{1... | collective-permute-start | bytes 491528 | tf_op jit(solution)/shard_map/ppermute | solution.py:217
  32.6 0.0 collective-permute-start.8
  32.6 0.0 collective-permute-done.6.refs_6_
  32.6 2.9 %collective-permute-start.11 = (f32[80,256]{1,0:T(8,128)S(1)}, f32[80,256]{1,0:T(8,128)S(1)}, u32[]{:S(2)}, u32[]{:S(2)}) collective-permute-start(f32[80,256]{1,0:T(8,128)S(1)} %collective-permute-done.6.refs_6_), channel_id=1, source_target_pairs={{0,16},{16,0},{32,48},{48,32},{64,80},{80,64},{96,112},{112,96},{1... | collective-permute-start | bytes 245768 | tf_op jit(solution)/shard_map/ppermute | solution.py:217
  35.5 0.0 collective-permute-start.9
  35.5 0.0 collective-permute-done.8.refs_8_
  35.5 0.9 collective-permute-done.11.refs_11_
  36.4 0.4 collective-permute-done.9.refs_9_
  36.8 0.0 collective-permute-done.7.refs_7_
  36.8 0.0 collective-permute-done.10.refs_10_
  36.8 3.8 %shard_map.70 = f32[1280,256]{1,0:T(8,128)S(1)} custom-call(s32[28]{0:T(128)S(1)} %get-tuple-element.20.sets_ref, bf16[1280,1280]{1,0:T(8,128)(2,1)S(1)} %get-tuple-element.21.high_ref, bf16[1280,1280]{1,0:T(8,128)(2,1)S(1)} %get-tuple-element.22.low_ref, f32[80,256]{1,0:T(8,128)S(1)} %collective-permute-done.refs_0_, ...), custom_call_target="tpu_custom_call" | custom-call | flops 2516582400 | bytes 9175040 | tf_op jit(solution)/shard_map/pallas_call | solution.py:219
  40.6 0.0 copy-start.1
  40.6 24.9 %all_to_all.20.parts_ref = f32[16,80,256]{2,1,0:T(8,128)S(1)} all-to-all(f32[16,80,256]{2,1,0:T(8,128)S(1)} %bitcast.3), channel_id=1, replica_groups=mesh['prow'=16,'pcol'=16] {'pcol'}, dimensions={0} | all-to-all | bytes 2621440 | tf_op jit(solution)/shard_map/all_to_all | solution.py:230
  65.5 0.0 copy-done
  65.5 0.9 shard_map.71
  66.4 1.4 %collective-permute-start.12 = (f32[256,256]{1,0:T(8,128)S(1)}, f32[256,256]{1,0:T(8,128)S(1)}, u32[]{:S(2)}, u32[]{:S(2)}) collective-permute-start(f32[256,256]{1,0:T(8,128)S(1)} %get-tuple-element.27), channel_id=1, source_target_pairs={{0,16},{16,0},{32,48},{48,32},{64,80},{80,64},{96,112},{112,96},{1... | collective-permute-start | bytes 786440 | tf_op jit(solution)/shard_map/ppermute | solution.py:250
  67.8 0.8 shard_map.72
  68.6 0.3 collective-permute-done.12
  69.0 10.8 %all_to_all.21 = f32[16,16,256]{2,1,0:T(8,128)S(1)} all-to-all(f32[16,16,256]{2,1,0:T(8,128)S(1)} %bitcast.6), channel_id=1, replica_groups=mesh['prow'=16,'pcol'=16] {'pcol'}, dimensions={0} | all-to-all | bytes 524288 | tf_op jit(solution)/shard_map/all_to_all | solution.py:251
  79.8 12.7 %all_to_all.22 = f32[8,16,256]{2,1,0:T(8,128)S(1)} all-to-all(f32[8,16,256]{2,1,0:T(8,128)S(1)} %broadcast_in_dim.4), channel_id=1, replica_groups={{0,32,64,96,128,160,192,224},{16,48,80,112,144,176,208,240},{1,33,65,97..., dimensions={0} | all-to-all | bytes 262144 | tf_op jit(solution)/shard_map/all_to_all | solution.py:253
  92.5 10.1 %all_to_all.23 = f32[16,16,256]{2,1,0:T(8,128)S(1)} all-to-all(f32[16,16,256]{2,1,0:T(8,128)S(1)} %broadcast_in_dim.5), channel_id=1, replica_groups=mesh['prow'=16,'pcol'=16] {'pcol'}, dimensions={0} | all-to-all | bytes 524288 | tf_op jit(solution)/shard_map/all_to_all | solution.py:255
  102.7 4.4 %collective-permute-start.13 = (f32[256,256]{1,0:T(8,128)S(1)}, f32[256,256]{1,0:T(8,128)S(1)}, u32[]{:S(2)}, u32[]{:S(2)}) collective-permute-start(f32[256,256]{1,0:T(8,128)S(1)} %bitcast.4), channel_id=1, source_target_pairs={{0,16},{16,0},{32,48},{48,32},{64,80},{80,64},{96,112},{112,96},{1... | collective-permute-start | bytes 786440 | tf_op jit(solution)/shard_map/ppermute | solution.py:256
  107.1 1.2 %shard_map.73 = f32[80,512]{1,0:T(8,128)} custom-call(s32[28]{0:T(128)S(1)} %get-tuple-element.20.sets_ref, f32[80,256]{1,0:T(8,128)S(1)} %get-tuple-element.28.y_ref), custom_call_target="tpu_custom_call" | custom-call | tf_op jit(solution)/shard_map/pallas_call | solution.py:258
  108.3 0.0 collective-permute-done.13.there_ref
  108.3 0.0 copy-done.1
  108.3 0.9 shard_map.74
  (7 shorter events, 0.1 us)
Async XLA Ops:
  2.2 13.8 %collective-permute-start = (f32[80,256]{1,0:T(8,128)}, f32[80,256]{1,0:T(8,128)S(1)}, u32[]{:S(2)}, u32[]{:S(2)}) collective-permute-start(f32[80,256]{1,0:T(8,128)} %shard_map.68.z_ref), channel_id=1, source_target_pairs={{10,0},{6,16},{9,32},{11,48},{5,64},{7,80},{15,96},{1,112},{12,128... | collective-permute-start | bytes 245768 | tf_op jit(solution)/shard_map/ppermute | solution.py:189
  11.1 0.7 copy-start.2
  11.8 0.7 copy-start.3
  16.0 3.5 %collective-permute-start.1 = (f32[80,256]{1,0:T(8,128)S(1)}, f32[80,256]{1,0:T(8,128)S(1)}, u32[]{:S(2)}, u32[]{:S(2)}) collective-permute-start(f32[80,256]{1,0:T(8,128)S(1)} %collective-permute-done.refs_0_), channel_id=1, source_target_pairs={{0,16},{16,0},{32,48},{48,32},{64,80},{80,64},{96,112},{112,96},{1... | collective-permute-start | bytes 245768 | tf_op jit(solution)/shard_map/ppermute | solution.py:209
  16.1 6.4 %collective-permute-start.2 = (f32[80,256]{1,0:T(8,128)S(1)}, f32[80,256]{1,0:T(8,128)S(1)}, u32[]{:S(2)}, u32[]{:S(2)}) collective-permute-start(f32[80,256]{1,0:T(8,128)S(1)} %collective-permute-done.refs_0_), channel_id=1, source_target_pairs={{0,64},{16,208},{32,96},{48,240},{64,128},{80,16},{96,160},{112,48... | collective-permute-start | bytes 245768 | tf_op jit(solution)/shard_map/ppermute | solution.py:207
  19.5 6.9 %collective-permute-start.4 = (f32[80,256]{1,0:T(8,128)S(1)}, f32[80,256]{1,0:T(8,128)S(1)}, u32[]{:S(2)}, u32[]{:S(2)}) collective-permute-start(f32[80,256]{1,0:T(8,128)S(1)} %collective-permute-done.1.refs_1_), channel_id=1, source_target_pairs={{0,64},{16,208},{32,96},{48,240},{64,128},{80,16},{96,160},{112,48... | collective-permute-start | bytes 245768 | tf_op jit(solution)/shard_map/ppermute | solution.py:207
  22.5 6.6 %collective-permute-start.3 = (f32[160,256]{1,0:T(8,128)S(1)}, f32[160,256]{1,0:T(8,128)S(1)}, u32[]{:S(2)}, u32[]{:S(2)}) collective-permute-start(f32[160,256]{1,0:T(8,128)S(1)} %pad_maximum_fusion), channel_id=1, source_target_pairs={{0,32},{16,240},{32,64},{48,16},{64,96},{80,48},{96,128},{112,80},... | collective-permute-start | bytes 491528 | tf_op jit(solution)/shard_map/ppermute | solution.py:207
  26.4 39.1 %copy-start = (f32[80,256]{1,0:T(8,128)S(1)}, f32[80,256]{1,0:T(8,128)}, u32[]{:S(2)}) copy-start(f32[80,256]{1,0:T(8,128)} %shard_map.68.z_ref) | copy-start | bytes 245764
  26.4 4.5 %collective-permute-start.5 = (f32[160,256]{1,0:T(8,128)S(1)}, f32[160,256]{1,0:T(8,128)S(1)}, u32[]{:S(2)}, u32[]{:S(2)}) collective-permute-start(f32[160,256]{1,0:T(8,128)S(1)} %pad_maximum_fusion.1), channel_id=1, source_target_pairs={{0,32},{16,240},{32,64},{48,16},{64,96},{80,48},{96,128},{112,80},... | collective-permute-start | bytes 491528 | tf_op jit(solution)/shard_map/ppermute | solution.py:207
  27.4 5.2 %collective-permute-start.6 = (f32[80,256]{1,0:T(8,128)S(1)}, f32[80,256]{1,0:T(8,128)S(1)}, u32[]{:S(2)}, u32[]{:S(2)}) collective-permute-start(f32[80,256]{1,0:T(8,128)S(1)} %collective-permute-done.2.refs_3_), channel_id=1, source_target_pairs={{0,64},{16,208},{32,96},{48,240},{64,128},{80,16},{96,160},{112,48... | collective-permute-start | bytes 245768 | tf_op jit(solution)/shard_map/ppermute | solution.py:207
  29.0 7.7 %collective-permute-start.7 = (f32[160,256]{1,0:T(8,128)S(1)}, f32[160,256]{1,0:T(8,128)S(1)}, u32[]{:S(2)}, u32[]{:S(2)}) collective-permute-start(f32[160,256]{1,0:T(8,128)S(1)} %collective-permute-done.3.refs_2_), channel_id=1, source_target_pairs={{0,16},{16,0},{32,48},{48,32},{64,80},{80,64},{96,112},{112,96},{1... | collective-permute-start | bytes 491528 | tf_op jit(solution)/shard_map/ppermute | solution.py:217
  31.0 5.8 %collective-permute-start.10 = (f32[160,256]{1,0:T(8,128)S(1)}, f32[160,256]{1,0:T(8,128)S(1)}, u32[]{:S(2)}, u32[]{:S(2)}) collective-permute-start(f32[160,256]{1,0:T(8,128)S(1)} %collective-permute-done.5.refs_5_), channel_id=1, source_target_pairs={{0,16},{16,0},{32,48},{48,32},{64,80},{80,64},{96,112},{112,96},{1... | collective-permute-start | bytes 491528 | tf_op jit(solution)/shard_map/ppermute | solution.py:217
  32.6 2.9 %collective-permute-start.8 = (f32[80,256]{1,0:T(8,128)S(1)}, f32[80,256]{1,0:T(8,128)S(1)}, u32[]{:S(2)}, u32[]{:S(2)}) collective-permute-start(f32[80,256]{1,0:T(8,128)S(1)} %collective-permute-done.2.refs_3_), channel_id=1, source_target_pairs={{0,16},{16,0},{32,48},{48,32},{64,80},{80,64},{96,112},{112,96},{1... | collective-permute-start | bytes 245768 | tf_op jit(solution)/shard_map/ppermute | solution.py:217
  32.6 3.9 %collective-permute-start.11 = (f32[80,256]{1,0:T(8,128)S(1)}, f32[80,256]{1,0:T(8,128)S(1)}, u32[]{:S(2)}, u32[]{:S(2)}) collective-permute-start(f32[80,256]{1,0:T(8,128)S(1)} %collective-permute-done.6.refs_6_), channel_id=1, source_target_pairs={{0,16},{16,0},{32,48},{48,32},{64,80},{80,64},{96,112},{112,96},{1... | collective-permute-start | bytes 245768 | tf_op jit(solution)/shard_map/ppermute | solution.py:217
  35.5 1.3 %collective-permute-start.9 = (f32[80,256]{1,0:T(8,128)S(1)}, f32[80,256]{1,0:T(8,128)S(1)}, u32[]{:S(2)}, u32[]{:S(2)}) collective-permute-start(f32[80,256]{1,0:T(8,128)S(1)} %collective-permute-done.4.refs_4_), channel_id=1, source_target_pairs={{0,16},{16,0},{32,48},{48,32},{64,80},{80,64},{96,112},{112,96},{1... | collective-permute-start | bytes 245768 | tf_op jit(solution)/shard_map/ppermute | solution.py:217
  40.6 67.8 %copy-start.1 = (f32[2,256,256]{2,1,0:T(8,128)S(1)}, f32[2,256,256]{2,1,0:T(8,128)}, u32[]{:S(2)}) copy-start(f32[2,256,256]{2,1,0:T(8,128)} %d_ref.1) | copy-start | bytes 1572868
  66.4 2.5 %collective-permute-start.12 = (f32[256,256]{1,0:T(8,128)S(1)}, f32[256,256]{1,0:T(8,128)S(1)}, u32[]{:S(2)}, u32[]{:S(2)}) collective-permute-start(f32[256,256]{1,0:T(8,128)S(1)} %get-tuple-element.27), channel_id=1, source_target_pairs={{0,16},{16,0},{32,48},{48,32},{64,80},{80,64},{96,112},{112,96},{1... | collective-permute-start | bytes 786440 | tf_op jit(solution)/shard_map/ppermute | solution.py:250
  102.7 5.6 %collective-permute-start.13 = (f32[256,256]{1,0:T(8,128)S(1)}, f32[256,256]{1,0:T(8,128)S(1)}, u32[]{:S(2)}, u32[]{:S(2)}) collective-permute-start(f32[256,256]{1,0:T(8,128)S(1)} %bitcast.4), channel_id=1, source_target_pairs={{0,16},{16,0},{32,48},{48,32},{64,80},{80,64},{96,112},{112,96},{1... | collective-permute-start | bytes 786440 | tf_op jit(solution)/shard_map/ppermute | solution.py:256
